TPU v7x, 128 devices: a whole 4x4x4 slice. The times are simulated.
128 devices in a mesh: row: 8 (over x, core), col: 16 (over y, z).
Axes of the slice: x: 4, y: 4, z: 4, core: 2. Of those that a mesh axis runs over, the one named last changes fastest.
Arguments:
- factor: bfloat16 [65536, 256], P(('row', 'col')), may hold values from -6 to 6
- relation_cores: float32 [2, 256, 256], replicated, may hold values from -6 to 6
- block_coords: int32 [2, 8, 16, 2, 96], P(None, 'row', 'col'), may hold values from 0 to 63, as said below
- block_values: int32 [2, 8, 16, 96, 128, 128], P(None, 'row', 'col'), may hold values from 0 to 3
- block_counts: int32 [2, 8, 16], P(None, 'row', 'col'), may hold values from 12 to 96, as said below
Outputs:
- factor_next: bfloat16 [65536, 256], P(('row', 'col'))
- cores_next: float32 [2, 256, 256], replicated
Inputs may be any that keep to these rules, and one draw needn't show every extreme that they name: block_coords[k, r, c, 0, s] is a row block below 64 and block_coords[k, r, c, 1, s] a column block below 32; the 96 slots of one list name distinct blocks. Only the first block_counts[k, r, c] slots of a list are live; in every layer some grid cell has 96 live slots.
All inputs are finite; a program needn't handle non-finite values.
Results may differ from a plain program's by a relative error of at most 0.0054.
Values may be sent and summed in bfloat16 or wider, within the bound.
A program may use at most 192 MiB of HBM per device.

v0:
```python
import math

import jax
import jax.numpy as jnp
from jax import lax
from jax.sharding import PartitionSpec as P

step_factor = 0.25
step_core = 4.0


def residual_of(forward_rows, own_cols, block_data, live_mask):
    predicted = jnp.einsum(
        "gar,gbr->gab", forward_rows, own_cols, preferred_element_type=jnp.float32
    )
    return ((predicted - block_data) * live_mask[:, None, None]).astype(jnp.bfloat16)


def group_terms(row_slabs, col_slabs, block_data, live_mask, layer_index, rank_width):
    offset = (1 + layer_index) * rank_width
    own_rows = row_slabs[:, :, :rank_width]
    forward_rows = row_slabs[:, :, offset : offset + rank_width]
    own_cols = col_slabs[:, :, :rank_width]
    backward_cols = col_slabs[:, :, offset : offset + rank_width]
    residual = residual_of(forward_rows, own_cols, block_data, live_mask)
    shared = jnp.einsum(
        "gab,gbr->gar", residual, own_cols, preferred_element_type=jnp.float32
    ).astype(jnp.bfloat16)
    row_term = jnp.einsum(
        "gab,gbr->gar", residual, backward_cols, preferred_element_type=jnp.float32
    )
    col_term = jnp.einsum(
        "gab,gar->gbr", residual, forward_rows, preferred_element_type=jnp.float32
    )
    core_term = jnp.einsum("gar,gas->rs", own_rows, shared, preferred_element_type=jnp.float32) * (
        1.0 / rank_width
    )
    return (row_term, col_term, core_term)


def on_device(factor, relation_cores, block_coords, block_values, block_counts):
    n_row = lax.axis_size("row")
    n_col = lax.axis_size("col")
    rank_width = factor.shape[1]
    layers = relation_cores.shape[0]
    block_size = block_values.shape[-1]
    slot_count = block_values.shape[3]
    batch_slots = 8
    core_low = relation_cores.astype(jnp.bfloat16)
    inverse_rank = 1.0 / rank_width

    def widen_rows(piece_rows):
        products = [
            (
                jnp.dot(piece_rows, core_low[layer_index], preferred_element_type=jnp.float32)
                * inverse_rank
            ).astype(jnp.bfloat16)
            for layer_index in range(layers)
        ]
        return jnp.concatenate([piece_rows] + products, axis=1)

    def widen_cols(piece_rows):
        products = [
            (
                lax.dot_general(
                    piece_rows,
                    core_low[layer_index],
                    (((1,), (1,)), ((), ())),
                    preferred_element_type=jnp.float32,
                )
                * inverse_rank
            ).astype(jnp.bfloat16)
            for layer_index in range(layers)
        ]
        return jnp.concatenate([piece_rows] + products, axis=1)

    row_panel = widen_rows(lax.all_gather(factor, "col", axis=0, tiled=True))
    col_panel = widen_cols(lax.all_gather(factor, "row", axis=0, tiled=True))
    row_blocks = row_panel.reshape(-1, block_size, row_panel.shape[1])
    col_blocks = col_panel.reshape(-1, block_size, col_panel.shape[1])

    def slot_group(layer_index, group_index):
        coords = block_coords[layer_index, 0, 0]
        first_slot = group_index * batch_slots
        row_index = lax.dynamic_slice_in_dim(coords[0], first_slot, batch_slots)
        col_index = lax.dynamic_slice_in_dim(coords[1], first_slot, batch_slots)
        block_data = lax.dynamic_slice_in_dim(
            block_values[layer_index, 0, 0], first_slot, batch_slots, 0
        ).astype(jnp.float32)
        live_mask = (
            first_slot + jnp.arange(batch_slots, dtype=jnp.int32) < block_counts[layer_index, 0, 0]
        ).astype(jnp.float32)
        return (row_index, col_index, block_data, live_mask)

    row_grad = jnp.zeros((row_blocks.shape[0], block_size, rank_width), jnp.float32)
    col_grad = jnp.zeros((col_blocks.shape[0], block_size, rank_width), jnp.float32)
    core_parts = []
    for layer_index in range(layers):

        def group_step(group_index, running, layer_index=layer_index):
            row_acc, col_acc, core_acc = running
            row_index, col_index, block_data, live_mask = slot_group(layer_index, group_index)
            row_term, col_term, core_term = group_terms(
                row_blocks[row_index],
                col_blocks[col_index],
                block_data,
                live_mask,
                layer_index,
                rank_width,
            )
            return (
                row_acc.at[row_index].add(row_term),
                col_acc.at[col_index].add(col_term),
                core_acc + core_term,
            )

        row_grad, col_grad, core_layer = lax.fori_loop(
            0,
            (block_counts[layer_index, 0, 0] + batch_slots - 1) // batch_slots,
            group_step,
            (row_grad, col_grad, jnp.zeros((rank_width, rank_width), jnp.float32)),
        )
        core_parts.append(core_layer)
    row_share = lax.psum_scatter(
        row_grad.reshape(-1, rank_width), "col", scatter_dimension=0, tiled=True
    )
    col_share = lax.psum_scatter(
        col_grad.reshape(-1, rank_width), "row", scatter_dimension=0, tiled=True
    )
    core_total = lax.psum(jnp.stack(core_parts), ("row", "col"))
    factor_next = (factor.astype(jnp.float32) - step_factor * (row_share + col_share)).astype(
        jnp.bfloat16
    )
    cores_next = relation_cores - step_core / math.sqrt(n_row * n_col * slot_count) * core_total
    return (factor_next, cores_next)


def solution(mesh):
    placed = (
        P(("row", "col"), None),
        P(),
        P(None, "row", "col", None, None),
        P(None, "row", "col", None, None, None),
        P(None, "row", "col"),
    )
    return jax.shard_map(
        on_device,
        mesh=mesh,
        in_specs=placed,
        out_specs=(P(("row", "col"), None), P()),
        check_vma=False,
    )
```

profile of v0, /device:TPU:0, one launch (start us, length us, event | category | flops | bytes accessed | tf_op | source)
XLA Modules:
  0.0 838.1 jit_solution(11244576054443843357)
XLA Ops:
  13.6 24.3 %all-gather.5.cloned.1.call-done = bf16[4096,256]{0,1:T(8,128)(2,1)} async-done(((bf16[512,256]{0,1:T(8,128)(2,1)}), bf16[4096,256]{0,1:T(8,128)(2,1)}) %all-gather.5.cloned.1.call-update) | async-done | bytes 2097168 | tf_op jit(solution)/shard_map/all_gather | solution.py:78
  41.1 9.4 %pad_maximum_fusion.1 = bf16[4096,768]{0,1:T(8,128)(2,1)} fusion(bf16[4096,256]{0,1:T(8,128)(2,1)S(1)} %fusion.41, bf16[4096,256]{0,1:T(8,128)(2,1)S(1)} %fusion.40, bf16[4096,256]{0,1:T(8,128)(2,1)S(1)} %copy-done.1), kind=kLoop, calls=%fused_computation.67 | loop fusion | flops 18874368 | bytes 12582912 | tf_op jit(solution)/shard_map/concatenate | solution.py:75
  50.5 8.6 %copy.22 = bf16[4096,768]{1,0:T(8,128)(2,1)} copy(bf16[4096,768]{0,1:T(8,128)(2,1)} %pad_maximum_fusion.1) | data formatting | bytes 12582912 | tf_op jit(solution)/shard_map/while | solution.py:117
  59.1 39.5 %all-gather.3.cloned.1.call-done = bf16[8192,256]{0,1:T(8,128)(2,1)} async-done(((bf16[512,256]{0,1:T(8,128)(2,1)}), bf16[8192,256]{0,1:T(8,128)(2,1)}) %all-gather.3.cloned.1.call-update) | async-done | bytes 4194320 | tf_op jit(solution)/shard_map/all_gather | solution.py:77
  98.7 3.6 fusion.38
  103.6 12.7 %pad_maximum_fusion = bf16[8192,768]{0,1:T(8,128)(2,1)} fusion(bf16[8192,256]{0,1:T(8,128)(2,1)S(1)} %fusion.39, bf16[8192,256]{0,1:T(8,128)(2,1)S(1)} %fusion.38, bf16[8192,256]{0,1:T(8,128)(2,1)S(1)} %copy-done), kind=kLoop, calls=%fused_computation.62 | loop fusion | flops 37748736 | bytes 25165824 | tf_op jit(solution)/shard_map/concatenate | solution.py:60
  116.3 16.6 %copy.21 = bf16[8192,768]{1,0:T(8,128)(2,1)} copy(bf16[8192,768]{0,1:T(8,128)(2,1)} %pad_maximum_fusion) | data formatting | bytes 25165824 | tf_op jit(solution)/shard_map/while | solution.py:117
  132.9 4.2 broadcast_in_dim.4
  139.7 98.0 %while.28 = (s32[]{:T(128)}, f32[64,128,256]{2,1,0:T(8,128)}, f32[32,128,256]{2,1,0:T(8,128)}, f32[256,256]{1,0:T(8,128)S(1)}, s32[]{:T(128)}, /*index=5*/s32[2,...) while((s32[]{:T(128)}, f32[64,128,256]{2,1,0:T(8,128)}, ...), condition=%wide.region_3.4_spmd, body=%wide.region_0.3_spmd.sunk | while | flops 404097088 | bytes 32516644 | solution.py:117
  140.0 3.4 gather_fusion
  143.4 6.4 gather_fusion.1
  159.4 3.4 scatter_fusion.1
  164.4 3.4 gather_fusion
  167.9 6.4 gather_fusion.1
  179.2 3.4 scatter_fusion
  188.9 3.4 gather_fusion
  192.4 6.4 gather_fusion.1
  213.4 3.4 gather_fusion
  216.8 6.4 gather_fusion.1
  237.7 102.6 %while.29 = (s32[]{:T(128)}, f32[64,128,256]{2,1,0:T(8,128)}, f32[32,128,256]{2,1,0:T(8,128)}, f32[256,256]{1,0:T(8,128)S(1)}, s32[]{:T(128)}, /*index=5*/s32[2,...) while((s32[]{:T(128)}, f32[64,128,256]{2,1,0:T(8,128)}, ...), condition=%wide.region_7.8_spmd, body=%wide.region_4.7_spmd.sunk | while | flops 404097088 | bytes 32516652 | solution.py:117
  237.9 3.4 gather_fusion.2
  241.3 6.4 gather_fusion.3
  263.5 3.4 gather_fusion.2
  267.0 6.4 gather_fusion.3
  289.1 3.4 gather_fusion.2
  292.6 6.4 gather_fusion.3
  314.7 3.4 gather_fusion.2
  318.2 6.4 gather_fusion.3
  330.6 3.4 scatter_fusion.2
  342.3 360.2 %all-reduce.2.cloned.1.call-done = f32[2,256,256]{2,1,0:T(8,128)} async-done(((f32[2,256,256]{2,1,0:T(8,128)}), f32[2,256,256]{2,1,0:T(8,128)}) %all-reduce.2.cloned.1.call-update) | async-done | bytes 524304 | tf_op jit(solution)/shard_map/psum | solution.py:130
  704.5 37.6 %reduce-scatter.5.cloned.1.call-done = f32[512,256]{1,0:T(8,128)} async-done(((f32[4096,256]{1,0:T(8,128)}), f32[512,256]{1,0:T(8,128)}) %reduce-scatter.5.cloned.1.call-update) | async-done | bytes 524304 | tf_op jit(solution)/shard_map/reduce_scatter | solution.py:127
  742.1 87.5 %reduce-scatter.3.cloned.1.call-done = f32[512,256]{1,0:T(8,128)} async-done(((f32[8192,256]{1,0:T(8,128)}), f32[512,256]{1,0:T(8,128)}) %reduce-scatter.3.cloned.1.call-update) | async-done | bytes 524304 | tf_op jit(solution)/shard_map/reduce_scatter | solution.py:124
  (131 shorter events, 129.0 us)
Async XLA Ops:
  7.2 30.7 %all-gather.5.cloned.1.call-start = ((), (), s32[]{:S(2)}) async-start(), calls=%async_computation.3 | async-start | bytes 2359296 | tf_op jit(solution)/shard_map/all_gather | solution.py:78
  9.0 89.6 %all-gather.3.cloned.1.call-start = ((), (), s32[]{:S(2)}) async-start(), calls=%async_computation.2 | async-start | bytes 4456448 | tf_op jit(solution)/shard_map/all_gather | solution.py:77
  9.8 692.8 %all-reduce.2.cloned.1.call-start = ((), (), s32[]{:S(2)}) async-start(), calls=%async_computation.6 | async-start | bytes 1048576 | tf_op jit(solution)/shard_map/psum | solution.py:130
  37.9 2.5 copy-start.1
  98.7 3.6 copy-start
  137.2 2.5 copy-start.4
  137.2 2.5 copy-start.5
  341.2 400.9 %reduce-scatter.5.cloned.1.call-start = ((), (), s32[]{:S(2)}) async-start(), calls=%async_computation.5 | async-start | bytes 4718592 | tf_op jit(solution)/shard_map/reduce_scatter | solution.py:127
  341.7 487.9 %reduce-scatter.3.cloned.1.call-start = ((), (), s32[]{:S(2)}) async-start(), calls=%async_computation.4 | async-start | bytes 8912896 | tf_op jit(solution)/shard_map/reduce_scatter | solution.py:124
  341.8 360.8 %copy-start.2 = (f32[2,256,256]{2,1,0:T(8,128)S(1)}, f32[2,256,256]{2,1,0:T(8,128)}, u32[]{:S(2)}) copy-start(f32[2,256,256]{2,1,0:T(8,128)} %param.10) | copy-start | bytes 1572868
  341.8 487.8 %copy-start.3 = (bf16[512,256]{1,0:T(8,128)(2,1)S(1)}, bf16[512,256]{1,0:T(8,128)(2,1)}, u32[]{:S(2)}) copy-start(bf16[512,256]{1,0:T(8,128)(2,1)} %param.9) | copy-start | bytes 786436
Sparse Core Ops, SparseCore 0:
  10.3 27.5 all-gather.4
  40.6 58.0 all-gather.2
  341.3 361.2 all-reduce.1
  705.0 37.1 reduce-scatter.4
  745.7 83.8 reduce-scatter.2
where the time goes:
time: 844 us; the launch traced here: 838 us
  waiting for transfers between devices  551 us (65%)
  local copies, waits for them, and re-layouts  142 us (17%)
  other arithmetic  84.4 us (10%)
  matrix products  44.8 us (5%)
  between operations  15.2 us (2%)
    psum x1, waiting for transfers between devices, on_device(): core_total = lax.psum(jnp.stack(core_parts), ('row', 'col'))  360 us
    reduce_scatter x1, waiting for transfers between devices, on_device(): lax.psum_scatter(row_grad.reshape(-1, rank_width), 'col', scatter_dimensi...  87.5 us
    gather x8, local copies, waits for them, and re-layouts, group_step(): row_blocks[row_index]  51 us
    all_gather x1, waiting for transfers between devices, on_device(): row_panel = widen_rows(lax.all_gather(factor, 'col', axis=0, tiled=True))  39.5 us
    reduce_scatter x1, waiting for transfers between devices, on_device(): lax.psum_scatter(col_grad.reshape(-1, rank_width), 'row', scatter_dimensi...  37.6 us
    gather x8, local copies, waits for them, and re-layouts, group_step(): col_blocks[col_index]  27.5 us
    scatter-add x8, other arithmetic, group_step(): row_acc.at[row_index].add(row_term)  26.5 us
    scatter-add x8, other arithmetic, group_step(): col_acc.at[col_index].add(col_term)  26.5 us
  transfers between devices with their start and end apart: 5, of which 5 were waited for; matrix products, arithmetic and copies ran while one was open for 3% of the time, Pallas kernels for 0%

commit v1 on v0

v1 whole, which is shorter than its diff:
```python
import math

import jax
import jax.numpy as jnp
from jax import lax
from jax.experimental import pallas as pl
from jax.experimental.pallas import tpu as pltpu
from jax.sharding import PartitionSpec as P

step_factor = 0.25
step_core = 4.0

RING = 4
GROUP = 4
DEPTH = 4
MESH = pl.DeviceIdType.MESH


class Place:
    def __init__(self):
        row = lax.axis_index("row")
        col = lax.axis_index("col")
        self.x, self.core = lax.div(row, 2), lax.rem(row, 2)
        self.y, self.z = lax.div(col, RING), lax.rem(col, RING)

    def shifted(self, dx=0, dy=0, dz=0, dcore=0):
        x = lax.rem(self.x + dx + RING, RING)
        y = lax.rem(self.y + dy + RING, RING)
        z = lax.rem(self.z + dz + RING, RING)
        core = lax.rem(self.core + dcore, 2)
        return x, y, z, core

    def device(self, **shift):
        x, y, z, core = self.shifted(**shift)
        return (x * 2 + core, y * RING + z)

    def row_piece(self, **shift):
        _, y, z, _ = self.shifted(**shift)
        return y * RING + z

    def col_piece(self, **shift):
        x, _, _, core = self.shifted(**shift)
        return x * 2 + core


def axes_of(half, a, b):
    return {"dy": a, "dz": b} if half == 0 else {"dy": b, "dz": a}


class Copies:
    def __init__(self, send_sems, recv_sems, local_sems):
        self.send_sems, self.recv_sems, self.local_sems = send_sems, recv_sems, local_sems
        self.sent, self.kept = [], 0

    def send(self, src, dst, device):
        number = len(self.sent)
        copy = pltpu.make_async_remote_copy(
            src_ref=src,
            dst_ref=dst,
            send_sem=self.send_sems.at[number],
            recv_sem=self.recv_sems.at[number],
            device_id=device,
            device_id_type=MESH,
        )
        copy.start()
        self.sent.append(copy)
        return copy

    def local(self, src, dst):
        copy = pltpu.make_async_copy(src, dst, self.local_sems.at[self.kept])
        self.kept += 1
        copy.start()
        return copy

    def finish(self):
        for copy in self.sent:
            copy.wait_send()


def greet(devices):
    barrier = pltpu.get_barrier_semaphore()
    for device in devices:
        pl.semaphore_signal(barrier, inc=1, device_id=device, device_id_type=MESH)
    pl.semaphore_wait(barrier, len(devices))


def rows(start, size):
    return pl.ds(pl.multiple_of(start, 16), size)


GATHER_SENDS = 40 + 8


def gather_kernel(factor_ref, row_ref, col_ref, send_sems, recv_sems, local_sems):
    here = Place()
    piece = factor_ref.shape[0]
    half_rows, part_rows = piece // 2, piece // 4
    links = Copies(send_sems, recv_sems, local_sems)
    greet(
        [here.device(dx=d) for d in (1, -1)]
        + [here.device(dy=d) for d in (1, -1)]
        + [here.device(dz=d) for d in (1, -1)]
        + [here.device(dcore=1)]
    )

    def region(half, a, b, part=None):
        start = here.row_piece(**axes_of(half, a, b)) * piece + half * half_rows
        if part is None:
            return row_ref.at[rows(start, half_rows)]
        return row_ref.at[rows(start + part * part_rows, part_rows)]

    def own(half):
        return factor_ref.at[pl.ds(half * half_rows, half_rows)]

    def col_region(dx, dcore, half=None):
        start = here.col_piece(dx=dx, dcore=dcore) * piece
        if half is None:
            return col_ref.at[rows(start, piece)]
        return col_ref.at[rows(start + half * half_rows, half_rows)]

    def first(half, sign):
        return here.device(**axes_of(half, sign, 0))

    def second(half, sign):
        return here.device(**axes_of(half, 0, sign))

    halves = (0, 1)
    along, ahead, back = {}, {}, {}
    for half in halves:
        for sign in (1, -1):
            along[half, sign] = links.send(own(half), region(half, 0, 0), first(half, sign))
        for sign in (1, -1):
            ahead[half, 0, sign] = links.send(own(half), region(half, 0, 0), second(half, sign))
    col_along = {
        sign: links.send(factor_ref, col_region(0, 0), here.device(dx=sign)) for sign in (1, -1)
    }
    sibling = here.device(dcore=1)
    across = [links.send(factor_ref, col_region(0, 0), sibling)]
    kept = [links.local(factor_ref, row_ref.at[rows(here.row_piece() * piece, piece)])]
    kept.append(links.local(factor_ref, col_region(0, 0)))

    def spread(half, a):
        for sign in (1, -1):
            ahead[half, a, sign] = links.send(region(half, a, 0), region(half, a, 0), second(half, sign))

    def pass_on(half, a):
        for sign in (1, -1):
            ahead[half, a, sign].wait_recv()
            part = 0 if sign == 1 else 1
            spot = region(half, a, -sign, part)
            back[half, a, sign] = links.send(spot, spot, second(half, sign))

    far = {}
    for sign in (1, -1):
        for half in halves:
            along[half, sign].wait_recv()
            part = 0 if sign == 1 else 1
            spot = region(half, -sign, 0, part)
            far[half, sign] = links.send(spot, spot, first(half, sign))
            spread(half, -sign)
    col_far = {}
    for sign in (1, -1):
        col_along[sign].wait_recv()
        spot = col_region(-sign, 0, 0 if sign == 1 else 1)
        col_far[sign] = links.send(spot, spot, here.device(dx=sign))
        across.append(links.send(col_region(-sign, 0), col_region(-sign, 0), sibling))
    for half in halves:
        pass_on(half, 0)
    for half in halves:
        for sign in (1, -1):
            far[half, sign].wait_recv()
        spread(half, 2)
    for sign in (1, -1):
        col_far[sign].wait_recv()
    across.append(links.send(col_region(2, 0), col_region(2, 0), sibling))
    for a in (-1, 1, 2):
        for half in halves:
            pass_on(half, a)
    for copy in back.values():
        copy.wait_recv()
    for copy in across:
        copy.wait_recv()
    for copy in kept:
        copy.wait()
    links.finish()


def gather(factor):
    piece, width = factor.shape
    return pl.pallas_call(
        gather_kernel,
        out_shape=(
            jax.ShapeDtypeStruct((RING * RING * piece, width), factor.dtype),
            jax.ShapeDtypeStruct((RING * 2 * piece, width), factor.dtype),
        ),
        in_specs=[pl.BlockSpec(memory_space=pl.ANY)],
        out_specs=(pl.BlockSpec(memory_space=pl.ANY), pl.BlockSpec(memory_space=pl.ANY)),
        scratch_shapes=[
            pltpu.SemaphoreType.DMA((GATHER_SENDS,)),
            pltpu.SemaphoreType.DMA((GATHER_SENDS,)),
            pltpu.SemaphoreType.DMA((2,)),
        ],
        compiler_params=pltpu.CompilerParams(collective_id=0, has_side_effects=True),
        name="gather_factor",
    )(factor)


def dot_nn(left, right):
    return jnp.dot(left, right, preferred_element_type=jnp.float32)


def dot_nt(left, right):
    return lax.dot_general(left, right, (((1,), (1,)), ((), ())), preferred_element_type=jnp.float32)


def dot_tn(left, right):
    return lax.dot_general(left, right, (((0,), (0,)), ((), ())), preferred_element_type=jnp.float32)


def block_kernel(
    coords_ref,
    counts_ref,
    cores_ref,
    row_hbm,
    col_hbm,
    values_hbm,
    row_out,
    col_out,
    core_out,
    row_all,
    col_all,
    forward,
    shared,
    col_acc,
    values,
    row_stage,
    col_stage,
    row_sems,
    col_sem,
    value_sems,
    out_sems,
):
    layers, rank, _ = cores_ref.shape
    block = values.shape[-1]
    total_rows, total_cols = row_all.shape[0], col_all.shape[0]
    inverse_rank = 1.0 / rank
    load_rows = total_rows // row_sems.shape[0]

    def row_load(index):
        spot = pl.ds(pl.multiple_of(index * load_rows, load_rows), load_rows)
        return pltpu.make_async_copy(row_hbm.at[spot], row_all.at[spot], row_sems.at[index])

    col_load = pltpu.make_async_copy(col_hbm, col_all, col_sem)
    for index in range(row_sems.shape[0]):
        row_load(index).start()
    col_load.start()

    groups = [(counts_ref[layer] + GROUP - 1) // GROUP for layer in range(layers)]
    total = groups[0] + groups[1]

    def slot_of(step):
        layer = (step >= groups[0]).astype(jnp.int32)
        return layer, (step - layer * groups[0]) * GROUP

    def value_load(step):
        layer, first_slot = slot_of(step)
        place = lax.rem(step, DEPTH)
        return pltpu.make_async_copy(
            values_hbm.at[layer, 0, 0, pl.ds(first_slot, GROUP)], values.at[place], value_sems.at[place]
        )

    for step in range(DEPTH - 1):
        value_load(jnp.int32(step)).start()

    low = [cores_ref[layer].astype(jnp.bfloat16) for layer in range(layers)]
    low_wide = jnp.concatenate(low, axis=1)

    @pl.loop(0, row_sems.shape[0])
    def _(index):
        row_load(index).wait()
        start = pl.multiple_of(index * load_rows, load_rows)
        product = dot_nn(row_all[pl.ds(start, load_rows)], low_wide) * inverse_rank
        for layer in range(layers):
            forward[pl.ds(layer * total_rows + start, load_rows)] = product[
                :, layer * rank : (layer + 1) * rank
            ].astype(jnp.bfloat16)
            shared[pl.ds(layer * total_rows + start, load_rows)] = jnp.zeros((load_rows, rank), jnp.float32)
        part = total_cols // row_sems.shape[0]
        col_acc[pl.ds(pl.multiple_of(index * part, part), part)] = jnp.zeros((part, rank), jnp.float32)

    col_load.wait()

    @pl.loop(0, total)
    def _(step):
        value_load(step).wait()

        @pl.when(step + DEPTH - 1 < total)
        def _():
            value_load(step + DEPTH - 1).start()

        layer, first_slot = slot_of(step)
        place = lax.rem(step, DEPTH)
        spots = []
        for slot in range(GROUP):
            row_block = coords_ref[layer * 2, first_slot + slot]
            col_block = coords_ref[layer * 2 + 1, first_slot + slot]
            row_start = pl.multiple_of(layer * total_rows + row_block * block, block)
            col_start = pl.multiple_of(col_block * block, block)
            spots.append((pl.ds(row_start, block), pl.ds(col_start, block)))
        residuals = []
        for slot in range(GROUP):
            row_spot, col_spot = spots[slot]
            predicted = dot_nt(forward[row_spot], col_all[col_spot])
            live = first_slot + slot < counts_ref[layer]
            residual = jnp.where(live, predicted - values[place, slot].astype(jnp.float32), 0.0)
            residuals.append(residual.astype(jnp.bfloat16))
        for slot in range(GROUP):
            row_spot, col_spot = spots[slot]
            shared[row_spot] += dot_nn(residuals[slot], col_all[col_spot])
            col_acc[col_spot] += dot_tn(residuals[slot], forward[row_spot])

    stage_rows = row_stage.shape[1]
    steps = total_rows // stage_rows
    core_out[...] = jnp.zeros_like(core_out)
    col_rows = total_cols // steps

    def row_store(index):
        place = lax.rem(index, 2)
        return pltpu.make_async_copy(
            row_stage.at[place],
            row_out.at[pl.ds(pl.multiple_of(index * stage_rows, stage_rows), stage_rows)],
            out_sems.at[place],
        )

    def col_store(index):
        place = lax.rem(index, 2)
        return pltpu.make_async_copy(
            col_stage.at[place],
            col_out.at[pl.ds(pl.multiple_of(index * col_rows, col_rows), col_rows)],
            out_sems.at[2 + place],
        )

    @pl.loop(0, steps)
    def _(index):
        place = lax.rem(index, 2)

        @pl.when(index >= 2)
        def _():
            row_store(index - 2).wait()
            col_store(index - 2).wait()

        start = pl.multiple_of(index * stage_rows, stage_rows)
        sums = [
            shared[pl.ds(layer * total_rows + start, stage_rows)].astype(jnp.bfloat16)
            for layer in range(layers)
        ]
        row_term = dot_nt(sums[0], low[0])
        for layer in range(1, layers):
            row_term += dot_nt(sums[layer], low[layer])
        row_stage[place] = (row_term * inverse_rank).astype(jnp.bfloat16)
        row_store(index).start()
        col_stage[place] = col_acc[pl.ds(pl.multiple_of(index * col_rows, col_rows), col_rows)].astype(
            jnp.bfloat16
        )
        col_store(index).start()
        own = row_all[pl.ds(start, stage_rows)]
        for layer in range(layers):
            core_out[pl.ds(layer * rank, rank)] += dot_tn(own, sums[layer])

    for index in (steps - 2, steps - 1):
        row_store(jnp.int32(index)).wait()
        col_store(jnp.int32(index)).wait()


def local_terms(coords, counts, cores, row_all, col_all, block_values):
    layers, rank, _ = cores.shape
    total_rows, total_cols = row_all.shape[0], col_all.shape[0]
    block = block_values.shape[-1]
    stage_rows = 1024
    steps = total_rows // stage_rows
    anywhere = pl.BlockSpec(memory_space=pl.ANY)
    return pl.pallas_call(
        block_kernel,
        out_shape=(
            jax.ShapeDtypeStruct((total_rows, rank), jnp.bfloat16),
            jax.ShapeDtypeStruct((total_cols, rank), jnp.bfloat16),
            jax.ShapeDtypeStruct((layers * rank, rank), jnp.float32),
        ),
        in_specs=[
            pl.BlockSpec(memory_space=pltpu.SMEM),
            pl.BlockSpec(memory_space=pltpu.SMEM),
            pl.BlockSpec(memory_space=pltpu.VMEM),
            anywhere,
            anywhere,
            anywhere,
        ],
        out_specs=(anywhere, anywhere, pl.BlockSpec(memory_space=pltpu.VMEM)),
        scratch_shapes=[
            pltpu.VMEM((total_rows, rank), jnp.bfloat16),
            pltpu.VMEM((total_cols, rank), jnp.bfloat16),
            pltpu.VMEM((layers * total_rows, rank), jnp.bfloat16),
            pltpu.VMEM((layers * total_rows, rank), jnp.float32),
            pltpu.VMEM((total_cols, rank), jnp.float32),
            pltpu.VMEM((DEPTH, GROUP, block, block), jnp.int32),
            pltpu.VMEM((2, stage_rows, rank), jnp.bfloat16),
            pltpu.VMEM((2, total_cols // steps, rank), jnp.bfloat16),
            pltpu.SemaphoreType.DMA((8,)),
            pltpu.SemaphoreType.DMA,
            pltpu.SemaphoreType.DMA((DEPTH,)),
            pltpu.SemaphoreType.DMA((4,)),
        ],
        compiler_params=pltpu.CompilerParams(vmem_limit_bytes=56 * 1024 * 1024),
        name="block_terms",
    )(coords, counts, cores, row_all, col_all, block_values)


REDUCE_SENDS = 60 + 10 + 20
REDUCE_LOCALS = 24 + 4 + 1
PASS, SIDE = {1: 0, -1: 1}, {1: 2, -1: 4}


def reduce_kernel(
    row_ref,
    col_ref,
    core_ref,
    grad_ref,
    core_total_ref,
    row_own,
    row_in,
    row_out,
    row_kept,
    col_own,
    col_pair,
    col_in,
    col_out,
    core_own,
    core_pair,
    core_x,
    core_y,
    core_z,
    core_mid,
    core_big,
    core_all,
    send_sems,
    recv_sems,
    local_sems,
):
    here = Place()
    piece, width = grad_ref.shape
    half_rows, part_rows = piece // 2, piece // 4
    links = Copies(send_sems, recv_sems, local_sems)
    others = [{"d" + axis: d} for axis in "xyz" for d in (1, 2, 3)]
    greet([here.device(**shift) for shift in others] + [here.device(dcore=1)])
    halves = (0, 1)

    def region(half, a, b, part=None):
        start = here.row_piece(**axes_of(half, a, b)) * piece + half * half_rows
        if part is None:
            return row_ref.at[rows(start, half_rows)]
        return row_ref.at[rows(start + part * part_rows, part_rows)]

    def first(half, sign):
        return here.device(**axes_of(half, sign, 0))

    def second(half, sign):
        return here.device(**axes_of(half, 0, sign))

    def wide(ref):
        return ref[...].astype(jnp.float32)

    def near(sign):
        return 0 if sign == 1 else 1

    sibling = here.device(dcore=1)
    rank = core_own.shape[0]

    other_layer = core_ref.at[rows((1 - here.core) * rank, rank)]
    core_swap = links.send(other_layer, core_pair, sibling)
    core_keep = links.local(core_ref.at[rows(here.core * rank, rank)], core_own)

    col_swap, col_keep = {}, {}
    for dx in (2, 1, -1, 0):
        slot = dx % RING
        spot = col_ref.at[rows(here.col_piece(dx=dx, dcore=1) * piece, piece)]
        col_swap[dx] = links.send(spot, col_pair.at[slot], sibling)
        spot = col_ref.at[rows(here.col_piece(dx=dx) * piece, piece)]
        col_keep[dx] = links.local(spot, col_own.at[slot])

    pass_in, side_in, kept = {}, {}, {}

    def send_far(a):
        for half in halves:
            for sign in (1, -1):
                pass_in[half, a, sign] = links.send(
                    region(half, a, 2, near(sign)), row_in.at[half, a % RING, PASS[sign]], second(half, sign)
                )

    def send_plain(a):
        for half in halves:
            for sign in (1, -1):
                part = 1 - near(sign)
                side_in[half, a, sign, part] = links.send(
                    region(half, a, sign, part), row_in.at[half, a % RING, SIDE[sign] + part], second(half, sign)
                )

    def load_own(a):
        for half in halves:
            for sign in (1, -1):
                part = near(sign)
                kept[half, a, sign] = links.local(
                    region(half, a, sign, part), row_own.at[half, a % RING, pl.ds(part * part_rows, part_rows)]
                )
            kept[half, a, 0] = links.local(
                region(half, a, 0), row_own.at[half, a % RING, pl.ds(half_rows, half_rows)]
            )

    def send_sum(a):
        for half in halves:
            for sign in (1, -1):
                part = near(sign)
                pass_in[half, a, sign].wait_recv()
                kept[half, a, sign].wait()
                arrived = wide(row_in.at[half, a % RING, PASS[sign]])
                mine = wide(row_own.at[half, a % RING, pl.ds(part * part_rows, part_rows)])
                out = row_out.at[half, a % RING, part]
                out[...] = (mine + arrived).astype(jnp.bfloat16)
                side_in[half, a, sign, part] = links.send(
                    out, row_in.at[half, a % RING, SIDE[sign] + part], second(half, sign)
                )

    def close(a):
        for half in halves:
            kept[half, a, 0].wait()
            for part in (0, 1):
                for sign in (1, -1):
                    side_in[half, a, sign, part].wait_recv()
                arrived = wide(row_in.at[half, a % RING, SIDE[1] + part]) + wide(
                    row_in.at[half, a % RING, SIDE[-1] + part]
                )
                mine = wide(row_own.at[half, a % RING, pl.ds(half_rows + part * part_rows, part_rows)])
                row_kept[half, a % RING, pl.ds(part * part_rows, part_rows)] = mine + arrived

    last_pass, last_in = {}, {}

    def last_out(half, slot, a, part):
        out = row_out.at[half, RING, slot]
        out[...] = row_kept[half, a % RING, pl.ds(part * part_rows, part_rows)].astype(jnp.bfloat16)
        return out

    def last_far():
        for half in halves:
            for sign in (1, -1):
                out = last_out(half, near(sign), 2, near(sign))
                last_pass[half, sign] = links.send(out, row_in.at[half, RING, PASS[sign]], first(half, sign))

    def last_plain(sign):
        for half in halves:
            part = 1 - near(sign)
            out = last_out(half, 2 + part, sign, part)
            last_in[half, sign, part] = links.send(
                out, row_in.at[half, RING, SIDE[sign] + part], first(half, sign)
            )

    def last_sum(sign):
        for half in halves:
            part = near(sign)
            last_pass[half, sign].wait_recv()
            total = row_kept[half, sign % RING, pl.ds(part * part_rows, part_rows)] + wide(
                row_in.at[half, RING, PASS[sign]]
            )
            out = row_out.at[half, RING, 4 + part]
            out[...] = total.astype(jnp.bfloat16)
            last_in[half, sign, part] = links.send(
                out, row_in.at[half, RING, SIDE[sign] + part], first(half, sign)
            )

    col_pass, col_side = {}, {}

    def col_sum(dx):
        col_swap[dx].wait_recv()
        col_keep[dx].wait()
        slot = dx % RING
        return wide(col_own.at[slot]) + wide(col_pair.at[slot])

    def half_of(part):
        return pl.ds(part * half_rows, half_rows)

    def col_far():
        col_out[0] = col_sum(2).astype(jnp.bfloat16)
        for sign in (1, -1):
            col_pass[sign] = links.send(
                col_out.at[0, half_of(near(sign))], col_in.at[PASS[sign]], here.device(dx=sign)
            )

    def col_plain(sign):
        total = col_sum(sign)
        slot = 1 if sign == 1 else 2
        col_own[sign % RING] = total.astype(jnp.bfloat16)
        part = 1 - near(sign)
        col_out[slot, half_of(part)] = total[part * half_rows : (part + 1) * half_rows].astype(jnp.bfloat16)
        col_side[sign, part] = links.send(
            col_out.at[slot, half_of(part)], col_in.at[SIDE[sign] + part], here.device(dx=sign)
        )

    def col_pass_on(sign):
        slot = 1 if sign == 1 else 2
        part = near(sign)
        col_pass[sign].wait_recv()
        pair = wide(col_own.at[sign % RING, half_of(part)])
        col_out[slot, half_of(part)] = (pair + wide(col_in.at[PASS[sign]])).astype(jnp.bfloat16)
        col_side[sign, part] = links.send(
            col_out.at[slot, half_of(part)], col_in.at[SIDE[sign] + part], here.device(dx=sign)
        )

    def col_close():
        total = col_sum(0)
        for part in (0, 1):
            for sign in (1, -1):
                col_side[sign, part].wait_recv()
            grad_ref[half_of(part)] = (
                total[part * half_rows : (part + 1) * half_rows]
                + wide(col_in.at[SIDE[1] + part])
                + wide(col_in.at[SIDE[-1] + part])
            )

    x_rows, y_rows = rank // RING, rank // RING // RING
    stage = {}

    def core_to_x():
        core_swap.wait_recv()
        core_keep.wait()
        core_own[...] += core_pair[...]
        for d in (2, 1, 3):
            chunk = lax.rem(here.x + d, RING)
            stage["x", d] = links.send(
                core_own.at[rows(chunk * x_rows, x_rows)], core_x.at[d], here.device(dx=d)
            )

    def core_to_y():
        for d in (1, 2, 3):
            stage["x", d].wait_recv()
        core_mid[...] = (
            core_own[rows(here.x * x_rows, x_rows)] + core_x[1] + core_x[2] + core_x[3]
        )
        for d in (2, 1, 3):
            chunk = lax.rem(here.y + d, RING)
            stage["y", d] = links.send(
                core_mid.at[rows(chunk * y_rows, y_rows)], core_y.at[d], here.device(dy=d)
            )

    def core_to_z():
        for d in (1, 2, 3):
            stage["y", d].wait_recv()
        core_z[here.z] = core_mid[rows(here.y * y_rows, y_rows)] + core_y[1] + core_y[2] + core_y[3]
        for d in (2, 1, 3):
            stage["z", d] = links.send(core_z.at[here.z], core_z.at[here.z], here.device(dz=d))

    def core_back_y():
        for d in (1, 2, 3):
            stage["z", d].wait_recv()
        spot = core_big.at[rows(here.x * x_rows + here.y * y_rows, y_rows)]
        spot[...] = (core_z[0] + core_z[1]) + (core_z[2] + core_z[3])
        for d in (2, 1, 3):
            stage["by", d] = links.send(spot, spot, here.device(dy=d))

    def core_back_x():
        for d in (1, 2, 3):
            stage["by", d].wait_recv()
        spot = core_big.at[rows(here.x * x_rows, x_rows)]
        for d in (2, 1, 3):
            stage["bx", d] = links.send(spot, spot, here.device(dx=d))

    def core_back_chip():
        for d in (1, 2, 3):
            stage["bx", d].wait_recv()
        stage["chip"] = links.send(core_big, core_all, sibling)

    def core_close():
        stage["chip"].wait_recv()
        core_total_ref[rows(here.core * rank, rank)] = core_big[...]
        core_total_ref[rows((1 - here.core) * rank, rank)] = core_all[...]

    send_far(2)
    send_far(1)
    send_plain(2)
    for a in (2, 1, -1, 0):
        load_own(a)
    core_to_x()
    col_far()
    col_plain(1)
    col_plain(-1)
    send_sum(2)
    send_far(-1)
    send_plain(1)
    core_to_y()
    send_sum(1)
    send_far(0)
    send_plain(-1)
    col_pass_on(1)
    col_pass_on(-1)
    close(2)
    last_far()
    core_to_z()
    send_sum(-1)
    send_plain(0)
    close(1)
    last_plain(1)
    core_back_y()
    send_sum(0)
    close(-1)
    last_plain(-1)
    core_back_x()
    last_sum(1)
    last_sum(-1)
    col_close()
    core_back_chip()
    close(0)
    core_close()
    for half in halves:
        for part in (0, 1):
            for sign in (1, -1):
                last_in[half, sign, part].wait_recv()
            spot = pl.ds(half * half_rows + part * part_rows, part_rows)
            grad_ref[spot] += (
                row_kept[half, 0, pl.ds(part * part_rows, part_rows)]
                + wide(row_in.at[half, RING, SIDE[1] + part])
                + wide(row_in.at[half, RING, SIDE[-1] + part])
            )
    links.finish()


def reduce(row_grad, col_grad, core_grad, piece):
    width = row_grad.shape[1]
    half_rows, part_rows = piece // 2, piece // 4
    rank = width
    low, full = jnp.bfloat16, jnp.float32
    anywhere = pl.BlockSpec(memory_space=pl.ANY)
    inside = pl.BlockSpec(memory_space=pltpu.VMEM)
    return pl.pallas_call(
        reduce_kernel,
        out_shape=(
            jax.ShapeDtypeStruct((piece, width), full),
            jax.ShapeDtypeStruct(core_grad.shape, full),
        ),
        in_specs=[anywhere] * 3,
        out_specs=(inside, inside),
        scratch_shapes=[
            pltpu.VMEM((2, RING, piece, width), low),
            pltpu.VMEM((2, RING + 1, 6, part_rows, width), low),
            pltpu.VMEM((2, RING + 1, 6, part_rows, width), low),
            pltpu.VMEM((2, RING, half_rows, width), full),
            pltpu.VMEM((RING, piece, width), low),
            pltpu.VMEM((RING, piece, width), low),
            pltpu.VMEM((6, half_rows, width), low),
            pltpu.VMEM((3, piece, width), low),
            pltpu.VMEM((rank, width), full),
            pltpu.VMEM((rank, width), full),
            pltpu.VMEM((RING, rank // 4, width), full),
            pltpu.VMEM((RING, rank // 16, width), full),
            pltpu.VMEM((RING, rank // 16, width), full),
            pltpu.VMEM((rank // 4, width), full),
            pltpu.VMEM((rank, width), full),
            pltpu.VMEM((rank, width), full),
            pltpu.SemaphoreType.DMA((REDUCE_SENDS,)),
            pltpu.SemaphoreType.DMA((REDUCE_SENDS,)),
            pltpu.SemaphoreType.DMA((REDUCE_LOCALS,)),
        ],
        compiler_params=pltpu.CompilerParams(
            collective_id=1, has_side_effects=True, vmem_limit_bytes=40 * 1024 * 1024
        ),
        name="reduce_terms",
    )(row_grad, col_grad, core_grad)


def on_device(factor, relation_cores, block_coords, block_values, block_counts):
    slot_count = block_values.shape[3]
    cells = lax.axis_size("row") * lax.axis_size("col")
    layers = relation_cores.shape[0]
    row_all, col_all = gather(factor)
    row_grad, col_grad, core_grad = local_terms(
        block_coords.reshape(layers * 2, slot_count),
        block_counts.reshape(layers),
        relation_cores,
        row_all,
        col_all,
        block_values,
    )
    gradient, core_total = reduce(row_grad, col_grad, core_grad, factor.shape[0])
    factor_next = (factor.astype(jnp.float32) - step_factor * gradient).astype(jnp.bfloat16)
    core_total = core_total.reshape(relation_cores.shape) * (1.0 / factor.shape[1])
    cores_next = relation_cores - step_core / math.sqrt(cells * slot_count) * core_total
    return (factor_next, cores_next)


def solution(mesh):
    placed = (
        P(("row", "col"), None),
        P(),
        P(None, "row", "col", None, None),
        P(None, "row", "col", None, None, None),
        P(None, "row", "col"),
    )
    return jax.shard_map(
        on_device,
        mesh=mesh,
        in_specs=placed,
        out_specs=(P(("row", "col"), None), P()),
        check_vma=False,
    )
```

time: 844 us -> 102 us (0.12)
  waiting for transfers between devices: 551 us -> 0 us
  local copies, waits for them, and re-layouts: 142 us -> 4.82 us
  Pallas kernels: 0 us -> 92.6 us
  other arithmetic: 84.4 us -> 1.66 us
  matrix products: 44.8 us -> 0 us
  between operations: 15.2 us -> 0.68 us
    psum x1 -> x0, waiting for transfers between devices: 360 us -> none  [on_device(): core_total = lax.psum(jnp.stack(core_parts), ('row', 'col'))]
    reduce_scatter x2 -> x0, waiting for transfers between devices: 125 us -> none  [the longest x1 87.5 us: on_device(): lax.psum_scatter(row_grad.reshape(-1, rank_width), 'col', scatter_dimensi...]
    pallas_call x0 -> x3, Pallas kernels: none -> 92.6 us  [the longest x1 35.6 us: reduce(): pl.pallas_call(reduce_kernel, out_shape=(jax.ShapeDtypeStruct((piece, wid...]
    gather x16 -> x0, local copies, waits for them, and re-layouts: 78.5 us -> none  [the longest x8 51 us: group_step(): row_blocks[row_index]]
    all_gather x2 -> x0, waiting for transfers between devices: 63.8 us -> none  [the longest x1 39.5 us: on_device(): row_panel = widen_rows(lax.all_gather(factor, 'col', axis=0, tiled=True))]
    scatter-add x16 -> x0, other arithmetic: 53 us -> none  [the longest x8 26.5 us: group_step(): row_acc.at[row_index].add(row_term)]
    dot_general x36 -> x0, matrix products: 44.8 us -> none  [the longest x8 12.6 us: group_terms(): jnp.einsum('gar,gas->rs', own_rows, shared, preferred_element_type=jnp.fl...]
    slice x21 -> x0, local copies, waits for them, and re-layouts: 29.4 us -> none  [the longest x8 25.7 us: slot_group(): block_values[layer_index, 0, 0]]
  transfers between devices with their start and end apart: 5 -> 0, of which waited for: 5 -> 0; matrix products, arithmetic and copies ran while one was open for 3% -> 0% of each run, Pallas kernels for 0% -> 0%
where the time goes in v1:
time: 102 us; the launch traced here: 99.7 us
  Pallas kernels  92.6 us (91%)
  local copies, waits for them, and re-layouts  4.82 us (5%)
  other arithmetic  1.66 us (2%)
    pallas_call x1, Pallas kernels, reduce(): pl.pallas_call(reduce_kernel, out_shape=(jax.ShapeDtypeStruct((piece, wid...  35.6 us
    pallas_call x1, Pallas kernels, gather(): pl.pallas_call(gather_kernel, out_shape=(jax.ShapeDtypeStruct((RING * RIN...  33.6 us
    pallas_call x1, Pallas kernels, local_terms(): pl.pallas_call(block_kernel, out_shape=(jax.ShapeDtypeStruct((total_rows,...  23.4 us
    unnamed x10, local copies, waits for them, and re-layouts  4.82 us

profile of v1, /device:TPU:0, one launch (start us, length us, event | category | flops | bytes accessed | tf_op | source)
XLA Modules:
  0.0 99.7 jit_solution(1383477830806121568)
XLA Ops:
  0.6 33.6 %gather_factor.1 = (bf16[8192,256]{1,0:T(8,128)(2,1)}, bf16[4096,256]{1,0:T(8,128)(2,1)}) custom-call(bf16[512,256]{1,0:T(8,128)(2,1)} %factor_ref.1), custom_call_target="tpu_custom_call" | custom-call | tf_op jit(solution)/shard_map/gather_factor/pallas_call | solution.py:190
  34.2 0.0 copy-start.4
  34.3 23.4 %block_terms.1 = (bf16[8192,256]{1,0:T(8,128)(2,1)}, bf16[4096,256]{1,0:T(8,128)(2,1)}, f32[512,256]{1,0:T(8,128)}) custom-call(s32[4,96]{1,0:T(4,128)} %bitcast.4, s32[2]{0:T(128)} %bitcast.5, f32[2,256,256]{2,1,0:T(8,128)} %cores_ref.1, bf16[8192,256]{1,0:T(8,128)(2,1)} %get-tuple-element.9.row_hbm, bf16[4096,256]{1,0:T(8,128)(2,1)} %get-tuple-element.10.col_hbm, ...), custom_call_target="tpu_custom_call" | custom-call | tf_op jit(solution)/shard_map/block_terms/pallas_call | solution.py:382
  57.6 0.0 copy-start
  57.6 2.2 %copy-done = bf16[8192,256]{1,0:T(8,128)(2,1)S(1)} copy-done((bf16[8192,256]{1,0:T(8,128)(2,1)S(1)}, bf16[8192,256]{1,0:T(8,128)(2,1)}, u32[]{:S(2)}) %copy-start) | copy-done | bytes 4194328
  59.8 0.0 copy-start.1
  59.8 1.6 %copy-done.1 = bf16[4096,256]{1,0:T(8,128)(2,1)S(1)} copy-done((bf16[4096,256]{1,0:T(8,128)(2,1)S(1)}, bf16[4096,256]{1,0:T(8,128)(2,1)}, u32[]{:S(2)}) %copy-start.1) | copy-done | bytes 2097176
  61.4 0.0 copy-start.2
  61.4 1.0 %copy-done.2 = f32[512,256]{1,0:T(8,128)S(1)} copy-done((f32[512,256]{1,0:T(8,128)S(1)}, f32[512,256]{1,0:T(8,128)}, u32[]{:S(2)}) %copy-start.2) | copy-done | bytes 524312
  62.4 0.0 copy-start.3
  62.4 35.6 %reduce_terms.1 = (f32[512,256]{1,0:T(8,128)S(1)}, f32[512,256]{1,0:T(8,128)S(1)}) custom-call(bf16[8192,256]{1,0:T(8,128)(2,1)S(1)} %copy-done, bf16[4096,256]{1,0:T(8,128)(2,1)S(1)} %copy-done.1, f32[512,256]{1,0:T(8,128)S(1)} %copy-done.2), custom_call_target="tpu_custom_call" | custom-call | tf_op jit(solution)/shard_map/reduce_terms/pallas_call | solution.py:739
  98.0 0.0 copy-done.4
  98.1 0.8 subtract_convert_fusion
  98.9 0.0 copy-done.3
  98.9 0.9 sub.7
Async XLA Ops:
  34.2 63.8 %copy-start.4 = (bf16[512,256]{1,0:T(8,128)(2,1)S(1)}, bf16[512,256]{1,0:T(8,128)(2,1)}, u32[]{:S(2)}) copy-start(bf16[512,256]{1,0:T(8,128)(2,1)} %factor_ref.1) | copy-start | bytes 786436
  57.6 2.2 %copy-start = (bf16[8192,256]{1,0:T(8,128)(2,1)S(1)}, bf16[8192,256]{1,0:T(8,128)(2,1)}, u32[]{:S(2)}) copy-start(bf16[8192,256]{1,0:T(8,128)(2,1)} %get-tuple-element.11.row_ref) | copy-start | bytes 12582916
  59.8 1.6 %copy-start.1 = (bf16[4096,256]{1,0:T(8,128)(2,1)S(1)}, bf16[4096,256]{1,0:T(8,128)(2,1)}, u32[]{:S(2)}) copy-start(bf16[4096,256]{1,0:T(8,128)(2,1)} %get-tuple-element.12.col_ref) | copy-start | bytes 6291460
  61.4 1.0 %copy-start.2 = (f32[512,256]{1,0:T(8,128)S(1)}, f32[512,256]{1,0:T(8,128)}, u32[]{:S(2)}) copy-start(f32[512,256]{1,0:T(8,128)} %get-tuple-element.13.core_ref) | copy-start | bytes 1572868
  62.4 36.4 %copy-start.3 = (f32[2,256,256]{2,1,0:T(8,128)S(1)}, f32[2,256,256]{2,1,0:T(8,128)}, u32[]{:S(2)}) copy-start(f32[2,256,256]{2,1,0:T(8,128)} %cores_ref.1) | copy-start | bytes 1572868

commit v2 on v1

--- a/solution.py
+++ b/solution.py
@@ -11,8 +11,8 @@
 step_core = 4.0
 
 RING = 4
-GROUP = 4
-DEPTH = 4
+GROUP = 16
+DEPTH = 3
 MESH = pl.DeviceIdType.MESH
 
 
@@ -41,6 +41,18 @@
     def col_piece(self, **shift):
         x, _, _, core = self.shifted(**shift)
         return x * 2 + core
+
+
+def dot_nn(left, right):
+    return jnp.dot(left, right, preferred_element_type=jnp.float32)
+
+
+def dot_nt(left, right):
+    return lax.dot_general(left, right, (((1,), (1,)), ((), ())), preferred_element_type=jnp.float32)
+
+
+def dot_tn(left, right):
+    return lax.dot_general(left, right, (((0,), (0,)), ((), ())), preferred_element_type=jnp.float32)
 
 
 def axes_of(half, a, b):
@@ -84,6 +96,10 @@
     pl.semaphore_wait(barrier, len(devices))
 
 
+def pinned(x):
+    return pltpu.with_memory_space_constraint(x, pltpu.VMEM)
+
+
 def rows(start, size):
     return pl.ds(pl.multiple_of(start, 16), size)
 
@@ -91,11 +107,27 @@
 GATHER_SENDS = 40 + 8
 
 
-def gather_kernel(factor_ref, row_ref, col_ref, send_sems, recv_sems, local_sems):
+def gather_kernel(
+    factor_ref,
+    cores_ref,
+    row_ref,
+    col_ref,
+    forward_ref,
+    shared_ref,
+    acc_ref,
+    cores,
+    low,
+    send_sems,
+    recv_sems,
+    local_sems,
+):
     here = Place()
     piece = factor_ref.shape[0]
     half_rows, part_rows = piece // 2, piece // 4
+    total_rows = row_ref.shape[0]
+    layers, rank, _ = cores_ref.shape
     links = Copies(send_sems, recv_sems, local_sems)
+    cores_in = links.local(cores_ref, cores)
     greet(
         [here.device(dx=d) for d in (1, -1)]
         + [here.device(dy=d) for d in (1, -1)]
@@ -139,6 +171,28 @@
     kept = [links.local(factor_ref, row_ref.at[rows(here.row_piece() * piece, piece)])]
     kept.append(links.local(factor_ref, col_region(0, 0)))
 
+    zero_rows = 512
+
+    @pl.loop(0, shared_ref.shape[0] // zero_rows)
+    def _(index):
+        shared_ref[rows(index * zero_rows, zero_rows)] = jnp.zeros((zero_rows, rank), jnp.float32)
+
+    @pl.loop(0, acc_ref.shape[0] // zero_rows)
+    def _(index):
+        acc_ref[rows(index * zero_rows, zero_rows)] = jnp.zeros((zero_rows, rank), jnp.float32)
+
+    cores_in.wait()
+    for layer in range(layers):
+        low[:, layer * rank : (layer + 1) * rank] = cores[layer].astype(jnp.bfloat16)
+
+    def widen(half, a, b):
+        start = here.row_piece(**axes_of(half, a, b)) * piece + half * half_rows
+        product = dot_nn(row_ref[rows(start, half_rows)], low[...]) * (1.0 / rank)
+        for layer in range(layers):
+            forward_ref[rows(layer * total_rows + start, half_rows)] = product[
+                :, layer * rank : (layer + 1) * rank
+            ].astype(jnp.bfloat16)
+
     def spread(half, a):
         for sign in (1, -1):
             ahead[half, a, sign] = links.send(region(half, a, 0), region(half, a, 0), second(half, sign))
@@ -150,6 +204,14 @@
             spot = region(half, a, -sign, part)
             back[half, a, sign] = links.send(spot, spot, second(half, sign))
 
+    def pass_wide(half, a):
+        for sign in (1, -1):
+            widen(half, a, -sign)
+
+    for copy in kept:
+        copy.wait()
+    for half in halves:
+        widen(half, 0, 0)
     far = {}
     for sign in (1, -1):
         for half in halves:
@@ -158,6 +220,9 @@
             spot = region(half, -sign, 0, part)
             far[half, sign] = links.send(spot, spot, first(half, sign))
             spread(half, -sign)
+    for sign in (1, -1):
+        for half in halves:
+            widen(half, -sign, 0)
     col_far = {}
     for sign in (1, -1):
         col_along[sign].wait_recv()
@@ -167,94 +232,77 @@
     for half in halves:
         pass_on(half, 0)
     for half in halves:
+        pass_wide(half, 0)
+    for half in halves:
         for sign in (1, -1):
             far[half, sign].wait_recv()
         spread(half, 2)
+    for half in halves:
+        widen(half, 2, 0)
     for sign in (1, -1):
         col_far[sign].wait_recv()
     across.append(links.send(col_region(2, 0), col_region(2, 0), sibling))
     for a in (-1, 1, 2):
         for half in halves:
             pass_on(half, a)
-    for copy in back.values():
-        copy.wait_recv()
+        for half in halves:
+            pass_wide(half, a)
+    for a in (0, -1, 1, 2):
+        for half in halves:
+            for sign in (1, -1):
+                back[half, a, sign].wait_recv()
+            widen(half, a, 2)
     for copy in across:
         copy.wait_recv()
-    for copy in kept:
-        copy.wait()
     links.finish()
 
 
-def gather(factor):
+def gather(factor, cores):
     piece, width = factor.shape
+    layers = cores.shape[0]
+    row_shape, col_shape = (RING * RING * piece, width), (RING * 2 * piece, width)
+    wide_shape = (layers * row_shape[0], width)
+    anywhere, inside = pl.BlockSpec(memory_space=pl.ANY), pl.BlockSpec(memory_space=pltpu.VMEM)
     return pl.pallas_call(
         gather_kernel,
         out_shape=(
-            jax.ShapeDtypeStruct((RING * RING * piece, width), factor.dtype),
-            jax.ShapeDtypeStruct((RING * 2 * piece, width), factor.dtype),
+            pltpu.VMEM(row_shape, factor.dtype),
+            pltpu.VMEM(col_shape, factor.dtype),
+            pltpu.VMEM(wide_shape, jnp.bfloat16),
+            pltpu.VMEM(wide_shape, jnp.float32),
+            pltpu.VMEM(col_shape, jnp.float32),
         ),
-        in_specs=[pl.BlockSpec(memory_space=pl.ANY)],
-        out_specs=(pl.BlockSpec(memory_space=pl.ANY), pl.BlockSpec(memory_space=pl.ANY)),
+        in_specs=[anywhere, anywhere],
+        out_specs=(inside,) * 5,
         scratch_shapes=[
+            pltpu.VMEM(cores.shape, jnp.float32),
+            pltpu.VMEM((width, layers * width), jnp.bfloat16),
             pltpu.SemaphoreType.DMA((GATHER_SENDS,)),
             pltpu.SemaphoreType.DMA((GATHER_SENDS,)),
-            pltpu.SemaphoreType.DMA((2,)),
+            pltpu.SemaphoreType.DMA((3,)),
         ],
-        compiler_params=pltpu.CompilerParams(collective_id=0, has_side_effects=True),
+        compiler_params=pltpu.CompilerParams(
+            collective_id=0, has_side_effects=True, vmem_limit_bytes=8 * 1024 * 1024
+        ),
         name="gather_factor",
-    )(factor)
-
-
-def dot_nn(left, right):
-    return jnp.dot(left, right, preferred_element_type=jnp.float32)
-
-
-def dot_nt(left, right):
-    return lax.dot_general(left, right, (((1,), (1,)), ((), ())), preferred_element_type=jnp.float32)
-
-
-def dot_tn(left, right):
-    return lax.dot_general(left, right, (((0,), (0,)), ((), ())), preferred_element_type=jnp.float32)
+    )(factor, cores)
 
 
 def block_kernel(
     coords_ref,
     counts_ref,
-    cores_ref,
-    row_hbm,
-    col_hbm,
+    forward,
+    col_all,
     values_hbm,
-    row_out,
-    col_out,
-    core_out,
-    row_all,
-    col_all,
-    forward,
+    shared_in,
+    acc_in,
     shared,
     col_acc,
     values,
-    row_stage,
-    col_stage,
-    row_sems,
-    col_sem,
     value_sems,
-    out_sems,
 ):
-    layers, rank, _ = cores_ref.shape
-    block = values.shape[-1]
-    total_rows, total_cols = row_all.shape[0], col_all.shape[0]
-    inverse_rank = 1.0 / rank
-    load_rows = total_rows // row_sems.shape[0]
-
-    def row_load(index):
-        spot = pl.ds(pl.multiple_of(index * load_rows, load_rows), load_rows)
-        return pltpu.make_async_copy(row_hbm.at[spot], row_all.at[spot], row_sems.at[index])
-
-    col_load = pltpu.make_async_copy(col_hbm, col_all, col_sem)
-    for index in range(row_sems.shape[0]):
-        row_load(index).start()
-    col_load.start()
-
+    layers, block = 2, values.shape[-1]
+    total_rows = forward.shape[0] // layers
     groups = [(counts_ref[layer] + GROUP - 1) // GROUP for layer in range(layers)]
     total = groups[0] + groups[1]
 
@@ -271,24 +319,6 @@
 
     for step in range(DEPTH - 1):
         value_load(jnp.int32(step)).start()
-
-    low = [cores_ref[layer].astype(jnp.bfloat16) for layer in range(layers)]
-    low_wide = jnp.concatenate(low, axis=1)
-
-    @pl.loop(0, row_sems.shape[0])
-    def _(index):
-        row_load(index).wait()
-        start = pl.multiple_of(index * load_rows, load_rows)
-        product = dot_nn(row_all[pl.ds(start, load_rows)], low_wide) * inverse_rank
-        for layer in range(layers):
-            forward[pl.ds(layer * total_rows + start, load_rows)] = product[
-                :, layer * rank : (layer + 1) * rank
-            ].astype(jnp.bfloat16)
-            shared[pl.ds(layer * total_rows + start, load_rows)] = jnp.zeros((load_rows, rank), jnp.float32)
-        part = total_cols // row_sems.shape[0]
-        col_acc[pl.ds(pl.multiple_of(index * part, part), part)] = jnp.zeros((part, rank), jnp.float32)
-
-    col_load.wait()
 
     @pl.loop(0, total)
     def _(step):
@@ -319,116 +349,43 @@
             shared[row_spot] += dot_nn(residuals[slot], col_all[col_spot])
             col_acc[col_spot] += dot_tn(residuals[slot], forward[row_spot])
 
-    stage_rows = row_stage.shape[1]
-    steps = total_rows // stage_rows
-    core_out[...] = jnp.zeros_like(core_out)
-    col_rows = total_cols // steps
-
-    def row_store(index):
-        place = lax.rem(index, 2)
-        return pltpu.make_async_copy(
-            row_stage.at[place],
-            row_out.at[pl.ds(pl.multiple_of(index * stage_rows, stage_rows), stage_rows)],
-            out_sems.at[place],
-        )
-
-    def col_store(index):
-        place = lax.rem(index, 2)
-        return pltpu.make_async_copy(
-            col_stage.at[place],
-            col_out.at[pl.ds(pl.multiple_of(index * col_rows, col_rows), col_rows)],
-            out_sems.at[2 + place],
-        )
-
-    @pl.loop(0, steps)
-    def _(index):
-        place = lax.rem(index, 2)
-
-        @pl.when(index >= 2)
-        def _():
-            row_store(index - 2).wait()
-            col_store(index - 2).wait()
-
-        start = pl.multiple_of(index * stage_rows, stage_rows)
-        sums = [
-            shared[pl.ds(layer * total_rows + start, stage_rows)].astype(jnp.bfloat16)
-            for layer in range(layers)
-        ]
-        row_term = dot_nt(sums[0], low[0])
-        for layer in range(1, layers):
-            row_term += dot_nt(sums[layer], low[layer])
-        row_stage[place] = (row_term * inverse_rank).astype(jnp.bfloat16)
-        row_store(index).start()
-        col_stage[place] = col_acc[pl.ds(pl.multiple_of(index * col_rows, col_rows), col_rows)].astype(
-            jnp.bfloat16
-        )
-        col_store(index).start()
-        own = row_all[pl.ds(start, stage_rows)]
-        for layer in range(layers):
-            core_out[pl.ds(layer * rank, rank)] += dot_tn(own, sums[layer])
-
-    for index in (steps - 2, steps - 1):
-        row_store(jnp.int32(index)).wait()
-        col_store(jnp.int32(index)).wait()
-
-
-def local_terms(coords, counts, cores, row_all, col_all, block_values):
-    layers, rank, _ = cores.shape
-    total_rows, total_cols = row_all.shape[0], col_all.shape[0]
+
+def local_terms(coords, counts, forward, col_all, block_values, shared, col_acc):
     block = block_values.shape[-1]
-    stage_rows = 1024
-    steps = total_rows // stage_rows
-    anywhere = pl.BlockSpec(memory_space=pl.ANY)
+    scalars, inside = pl.BlockSpec(memory_space=pltpu.SMEM), pl.BlockSpec(memory_space=pltpu.VMEM)
     return pl.pallas_call(
         block_kernel,
-        out_shape=(
-            jax.ShapeDtypeStruct((total_rows, rank), jnp.bfloat16),
-            jax.ShapeDtypeStruct((total_cols, rank), jnp.bfloat16),
-            jax.ShapeDtypeStruct((layers * rank, rank), jnp.float32),
-        ),
-        in_specs=[
-            pl.BlockSpec(memory_space=pltpu.SMEM),
-            pl.BlockSpec(memory_space=pltpu.SMEM),
-            pl.BlockSpec(memory_space=pltpu.VMEM),
-            anywhere,
-            anywhere,
-            anywhere,
+        out_shape=(pltpu.VMEM(shared.shape, jnp.float32), pltpu.VMEM(col_acc.shape, jnp.float32)),
+        in_specs=[scalars, scalars, inside, inside, pl.BlockSpec(memory_space=pl.ANY), inside, inside],
+        out_specs=(inside, inside),
+        input_output_aliases={5: 0, 6: 1},
+        scratch_shapes=[
+            pltpu.VMEM((DEPTH, GROUP, block, block), jnp.int32),
+            pltpu.SemaphoreType.DMA((DEPTH,)),
         ],
-        out_specs=(anywhere, anywhere, pl.BlockSpec(memory_space=pltpu.VMEM)),
-        scratch_shapes=[
-            pltpu.VMEM((total_rows, rank), jnp.bfloat16),
-            pltpu.VMEM((total_cols, rank), jnp.bfloat16),
-            pltpu.VMEM((layers * total_rows, rank), jnp.bfloat16),
-            pltpu.VMEM((layers * total_rows, rank), jnp.float32),
-            pltpu.VMEM((total_cols, rank), jnp.float32),
-            pltpu.VMEM((DEPTH, GROUP, block, block), jnp.int32),
-            pltpu.VMEM((2, stage_rows, rank), jnp.bfloat16),
-            pltpu.VMEM((2, total_cols // steps, rank), jnp.bfloat16),
-            pltpu.SemaphoreType.DMA((8,)),
-            pltpu.SemaphoreType.DMA,
-            pltpu.SemaphoreType.DMA((DEPTH,)),
-            pltpu.SemaphoreType.DMA((4,)),
-        ],
-        compiler_params=pltpu.CompilerParams(vmem_limit_bytes=56 * 1024 * 1024),
+        compiler_params=pltpu.CompilerParams(vmem_limit_bytes=12 * 1024 * 1024),
         name="block_terms",
-    )(coords, counts, cores, row_all, col_all, block_values)
+    )(coords, counts, forward, col_all, block_values, shared, col_acc)
 
 
 REDUCE_SENDS = 60 + 10 + 20
-REDUCE_LOCALS = 24 + 4 + 1
 PASS, SIDE = {1: 0, -1: 1}, {1: 2, -1: 4}
 
 
 def reduce_kernel(
+    shared_ref,
+    acc_ref,
     row_ref,
-    col_ref,
-    core_ref,
+    cores_ref,
     grad_ref,
     core_total_ref,
-    row_own,
+    cores,
+    low,
+    core_terms,
     row_in,
     row_out,
     row_kept,
+    col_swap_out,
     col_own,
     col_pair,
     col_in,
@@ -448,16 +405,29 @@
     here = Place()
     piece, width = grad_ref.shape
     half_rows, part_rows = piece // 2, piece // 4
+    total_rows = row_ref.shape[0]
+    layers, rank, _ = cores_ref.shape
     links = Copies(send_sems, recv_sems, local_sems)
+    cores_in = links.local(cores_ref, cores)
     others = [{"d" + axis: d} for axis in "xyz" for d in (1, 2, 3)]
     greet([here.device(**shift) for shift in others] + [here.device(dcore=1)])
     halves = (0, 1)
 
-    def region(half, a, b, part=None):
+    cores_in.wait()
+    for layer in range(layers):
+        low[layer] = cores[layer].astype(jnp.bfloat16)
+
+    def term(half, a, b, part=None):
         start = here.row_piece(**axes_of(half, a, b)) * piece + half * half_rows
-        if part is None:
-            return row_ref.at[rows(start, half_rows)]
-        return row_ref.at[rows(start + part * part_rows, part_rows)]
+        size = half_rows
+        if part is not None:
+            start, size = start + part * part_rows, part_rows
+        total = None
+        for layer in range(layers):
+            sums = shared_ref[rows(layer * total_rows + start, size)].astype(jnp.bfloat16)
+            product = dot_nt(sums, low[layer])
+            total = product if total is None else total + product
+        return total * (1.0 / rank)
 
     def first(half, sign):
         return here.device(**axes_of(half, sign, 0))
@@ -472,57 +442,37 @@
         return 0 if sign == 1 else 1
 
     sibling = here.device(dcore=1)
-    rank = core_own.shape[0]
-
-    other_layer = core_ref.at[rows((1 - here.core) * rank, rank)]
-    core_swap = links.send(other_layer, core_pair, sibling)
-    core_keep = links.local(core_ref.at[rows(here.core * rank, rank)], core_own)
-
-    col_swap, col_keep = {}, {}
-    for dx in (2, 1, -1, 0):
-        slot = dx % RING
-        spot = col_ref.at[rows(here.col_piece(dx=dx, dcore=1) * piece, piece)]
-        col_swap[dx] = links.send(spot, col_pair.at[slot], sibling)
-        spot = col_ref.at[rows(here.col_piece(dx=dx) * piece, piece)]
-        col_keep[dx] = links.local(spot, col_own.at[slot])
-
-    pass_in, side_in, kept = {}, {}, {}
+    pass_in, side_in, col_swap, stage = {}, {}, {}, {}
 
     def send_far(a):
         for half in halves:
+            both = term(half, a, 2).astype(jnp.bfloat16)
             for sign in (1, -1):
+                part = near(sign)
+                out = row_out.at[half, a % RING, PASS[sign]]
+                out[...] = both[part * part_rows : (part + 1) * part_rows]
                 pass_in[half, a, sign] = links.send(
-                    region(half, a, 2, near(sign)), row_in.at[half, a % RING, PASS[sign]], second(half, sign)
+                    out, row_in.at[half, a % RING, PASS[sign]], second(half, sign)
                 )
 
     def send_plain(a):
         for half in halves:
             for sign in (1, -1):
                 part = 1 - near(sign)
+                out = row_out.at[half, a % RING, SIDE[sign] + part]
+                out[...] = term(half, a, sign, part).astype(jnp.bfloat16)
                 side_in[half, a, sign, part] = links.send(
-                    region(half, a, sign, part), row_in.at[half, a % RING, SIDE[sign] + part], second(half, sign)
+                    out, row_in.at[half, a % RING, SIDE[sign] + part], second(half, sign)
                 )
 
-    def load_own(a):
+    def send_sum(a):
         for half in halves:
             for sign in (1, -1):
                 part = near(sign)
-                kept[half, a, sign] = links.local(
-                    region(half, a, sign, part), row_own.at[half, a % RING, pl.ds(part * part_rows, part_rows)]
-                )
-            kept[half, a, 0] = links.local(
-                region(half, a, 0), row_own.at[half, a % RING, pl.ds(half_rows, half_rows)]
-            )
-
-    def send_sum(a):
-        for half in halves:
-            for sign in (1, -1):
-                part = near(sign)
+                mine = term(half, a, sign, part)
                 pass_in[half, a, sign].wait_recv()
-                kept[half, a, sign].wait()
                 arrived = wide(row_in.at[half, a % RING, PASS[sign]])
-                mine = wide(row_own.at[half, a % RING, pl.ds(part * part_rows, part_rows)])
-                out = row_out.at[half, a % RING, part]
+                out = row_out.at[half, a % RING, SIDE[sign] + part]
                 out[...] = (mine + arrived).astype(jnp.bfloat16)
                 side_in[half, a, sign, part] = links.send(
                     out, row_in.at[half, a % RING, SIDE[sign] + part], second(half, sign)
@@ -530,15 +480,36 @@
 
     def close(a):
         for half in halves:
-            kept[half, a, 0].wait()
+            mine = term(half, a, 0)
             for part in (0, 1):
                 for sign in (1, -1):
                     side_in[half, a, sign, part].wait_recv()
                 arrived = wide(row_in.at[half, a % RING, SIDE[1] + part]) + wide(
                     row_in.at[half, a % RING, SIDE[-1] + part]
                 )
-                mine = wide(row_own.at[half, a % RING, pl.ds(half_rows + part * part_rows, part_rows)])
-                row_kept[half, a % RING, pl.ds(part * part_rows, part_rows)] = mine + arrived
+                row_kept[half, a % RING, pl.ds(part * part_rows, part_rows)] = (
+                    mine[part * part_rows : (part + 1) * part_rows] + arrived
+                )
+
+    def send_swap(dx):
+        slot = dx % RING
+        out = col_swap_out.at[slot]
+        out[...] = acc_ref[rows(here.col_piece(dx=dx, dcore=1) * piece, piece)].astype(jnp.bfloat16)
+        col_swap[dx] = links.send(out, col_pair.at[slot], sibling)
+
+    def core_start():
+        core_terms[...] = jnp.zeros_like(core_terms)
+        step_rows = 1024
+
+        @pl.loop(0, total_rows // step_rows)
+        def _(index):
+            start = index * step_rows
+            own = row_ref[rows(start, step_rows)]
+            for layer in range(layers):
+                sums = shared_ref[rows(layer * total_rows + start, step_rows)].astype(jnp.bfloat16)
+                core_terms[pl.ds(layer * rank, rank)] += dot_tn(own, sums)
+
+        stage["swap"] = links.send(core_terms.at[rows((1 - here.core) * rank, rank)], core_pair, sibling)
 
     last_pass, last_in = {}, {}
 
@@ -577,10 +548,9 @@
     col_pass, col_side = {}, {}
 
     def col_sum(dx):
+        mine = acc_ref[rows(here.col_piece(dx=dx) * piece, piece)]
         col_swap[dx].wait_recv()
-        col_keep[dx].wait()
-        slot = dx % RING
-        return wide(col_own.at[slot]) + wide(col_pair.at[slot])
+        return mine + wide(col_pair.at[dx % RING])
 
     def half_of(part):
         return pl.ds(part * half_rows, half_rows)
@@ -595,7 +565,8 @@
     def col_plain(sign):
         total = col_sum(sign)
         slot = 1 if sign == 1 else 2
-        col_own[sign % RING] = total.astype(jnp.bfloat16)
+        part = near(sign)
+        col_own[slot - 1] = total[part * half_rows : (part + 1) * half_rows]
         part = 1 - near(sign)
         col_out[slot, half_of(part)] = total[part * half_rows : (part + 1) * half_rows].astype(jnp.bfloat16)
         col_side[sign, part] = links.send(
@@ -606,8 +577,7 @@
         slot = 1 if sign == 1 else 2
         part = near(sign)
         col_pass[sign].wait_recv()
-        pair = wide(col_own.at[sign % RING, half_of(part)])
-        col_out[slot, half_of(part)] = (pair + wide(col_in.at[PASS[sign]])).astype(jnp.bfloat16)
+        col_out[slot, half_of(part)] = (col_own[slot - 1] + wide(col_in.at[PASS[sign]])).astype(jnp.bfloat16)
         col_side[sign, part] = links.send(
             col_out.at[slot, half_of(part)], col_in.at[SIDE[sign] + part], here.device(dx=sign)
         )
@@ -624,12 +594,10 @@
             )
 
     x_rows, y_rows = rank // RING, rank // RING // RING
-    stage = {}
 
     def core_to_x():
-        core_swap.wait_recv()
-        core_keep.wait()
-        core_own[...] += core_pair[...]
+        stage["swap"].wait_recv()
+        core_own[...] = core_terms[rows(here.core * rank, rank)] + core_pair[...]
         for d in (2, 1, 3):
             chunk = lax.rem(here.x + d, RING)
             stage["x", d] = links.send(
@@ -681,19 +649,21 @@
         core_total_ref[rows((1 - here.core) * rank, rank)] = core_all[...]
 
     send_far(2)
+    send_swap(2)
     send_far(1)
     send_plain(2)
-    for a in (2, 1, -1, 0):
-        load_own(a)
-    core_to_x()
+    for dx in (1, -1, 0):
+        send_swap(dx)
+    core_start()
     col_far()
     col_plain(1)
     col_plain(-1)
     send_sum(2)
+    core_to_x()
     send_far(-1)
     send_plain(1)
+    send_sum(1)
     core_to_y()
-    send_sum(1)
     send_far(0)
     send_plain(-1)
     col_pass_on(1)
@@ -729,8 +699,9 @@
     links.finish()
 
 
-def reduce(row_grad, col_grad, core_grad, piece):
-    width = row_grad.shape[1]
+def reduce(shared, col_acc, row_all, cores, piece):
+    width = row_all.shape[1]
+    layers = cores.shape[0]
     half_rows, part_rows = piece // 2, piece // 4
     rank = width
     low, full = jnp.bfloat16, jnp.float32
@@ -740,16 +711,19 @@
         reduce_kernel,
         out_shape=(
             jax.ShapeDtypeStruct((piece, width), full),
-            jax.ShapeDtypeStruct(core_grad.shape, full),
+            jax.ShapeDtypeStruct((layers * rank, width), full),
         ),
-        in_specs=[anywhere] * 3,
+        in_specs=[inside, inside, inside, anywhere],
         out_specs=(inside, inside),
         scratch_shapes=[
-            pltpu.VMEM((2, RING, piece, width), low),
+            pltpu.VMEM(cores.shape, full),
+            pltpu.VMEM(cores.shape, low),
+            pltpu.VMEM((layers * rank, width), full),
             pltpu.VMEM((2, RING + 1, 6, part_rows, width), low),
             pltpu.VMEM((2, RING + 1, 6, part_rows, width), low),
             pltpu.VMEM((2, RING, half_rows, width), full),
             pltpu.VMEM((RING, piece, width), low),
+            pltpu.VMEM((2, half_rows, width), full),
             pltpu.VMEM((RING, piece, width), low),
             pltpu.VMEM((6, half_rows, width), low),
             pltpu.VMEM((3, piece, width), low),
@@ -763,29 +737,33 @@
             pltpu.VMEM((rank, width), full),
             pltpu.SemaphoreType.DMA((REDUCE_SENDS,)),
             pltpu.SemaphoreType.DMA((REDUCE_SENDS,)),
-            pltpu.SemaphoreType.DMA((REDUCE_LOCALS,)),
+            pltpu.SemaphoreType.DMA((1,)),
         ],
         compiler_params=pltpu.CompilerParams(
-            collective_id=1, has_side_effects=True, vmem_limit_bytes=40 * 1024 * 1024
+            collective_id=1, has_side_effects=True, vmem_limit_bytes=28 * 1024 * 1024
         ),
         name="reduce_terms",
-    )(row_grad, col_grad, core_grad)
+    )(shared, col_acc, row_all, cores)
 
 
 def on_device(factor, relation_cores, block_coords, block_values, block_counts):
     slot_count = block_values.shape[3]
     cells = lax.axis_size("row") * lax.axis_size("col")
     layers = relation_cores.shape[0]
-    row_all, col_all = gather(factor)
-    row_grad, col_grad, core_grad = local_terms(
-        block_coords.reshape(layers * 2, slot_count),
-        block_counts.reshape(layers),
-        relation_cores,
-        row_all,
-        col_all,
-        block_values,
+    row_all, col_all, forward, shared, col_acc = map(pinned, gather(factor, relation_cores))
+    shared, col_acc = map(
+        pinned,
+        local_terms(
+            block_coords.reshape(layers * 2, slot_count),
+            block_counts.reshape(layers),
+            forward,
+            col_all,
+            block_values,
+            shared,
+            col_acc,
+        ),
     )
-    gradient, core_total = reduce(row_grad, col_grad, core_grad, factor.shape[0])
+    gradient, core_total = reduce(shared, col_acc, row_all, relation_cores, factor.shape[0])
     factor_next = (factor.astype(jnp.float32) - step_factor * gradient).astype(jnp.bfloat16)
     core_total = core_total.reshape(relation_cores.shape) * (1.0 / factor.shape[1])
     cores_next = relation_cores - step_core / math.sqrt(cells * slot_count) * core_total

time: 102 us -> 98.2 us (0.963)
  Pallas kernels: 92.6 us -> 79.4 us
  local copies, waits for them, and re-layouts: 4.82 us -> 14.8 us
    pallas_call x2, Pallas kernels: 57 us -> 37.7 us  [the longest x1 32.7 us: gather(): pl.pallas_call(gather_kernel, out_shape=(pltpu.VMEM(row_shape, factor.dty...]
    unnamed x10 -> x16, local copies, waits for them, and re-layouts: 4.82 us -> 14.8 us
    pallas_call x1, Pallas kernels: 35.6 us -> 41.7 us  [reduce(): pl.pallas_call(reduce_kernel, out_shape=(jax.ShapeDtypeStruct((piece, wid...]
where the time goes in v2:
time: 98.2 us; the launch traced here: 96.6 us
  Pallas kernels  79.4 us (81%)
  local copies, waits for them, and re-layouts  14.8 us (15%)
  other arithmetic  1.66 us (2%)
    pallas_call x1, Pallas kernels, reduce(): pl.pallas_call(reduce_kernel, out_shape=(jax.ShapeDtypeStruct((piece, wid...  41.7 us
    pallas_call x1, Pallas kernels, gather(): pl.pallas_call(gather_kernel, out_shape=(pltpu.VMEM(row_shape, factor.dty...  32.7 us
    unnamed x16, local copies, waits for them, and re-layouts  14.8 us
    pallas_call x1, Pallas kernels, local_terms(): pl.pallas_call(block_kernel, out_shape=(pltpu.VMEM(shared.shape, jnp.floa...  5.02 us

profile of v2, /device:TPU:0, one launch (start us, length us, event | category | flops | bytes accessed | tf_op | source)
XLA Modules:
  0.0 96.6 jit_solution(1287811403436582999)
XLA Ops:
  0.6 0.0 copy-start.2
  0.6 1.0 %copy-done.2 = f32[2,256,256]{2,1,0:T(8,128)S(1)} copy-done((f32[2,256,256]{2,1,0:T(8,128)S(1)}, f32[2,256,256]{2,1,0:T(8,128)}, u32[]{:S(2)}) %copy-start.2) | copy-done | bytes 524312
  1.7 0.0 copy-start.4
  1.7 0.9 copy-done.4
  2.6 32.7 %gather_factor.1 = (bf16[8192,256]{1,0:T(8,128)(2,1)S(1)}, bf16[4096,256]{1,0:T(8,128)(2,1)S(1)}, bf16[16384,256]{1,0:T(8,128)(2,1)S(1)}, f32[16384,256]{1,0:T(8,128)S(1)}, f32[4096,256]{1,0:T(8,128)S(1)}) custom-call(bf16[512,256]{1,0:T(8,128)(2,1)S(1)} %copy-done.4, f32[2,256,256]{2,1,0:T(8,128)S(1)} %copy-done.2), custom_call_target="tpu_custom_call" | custom-call | tf_op jit(solution)/shard_map/gather_factor/pallas_call | solution.py:266
  35.4 0.0 copy-start.6
  35.4 0.7 copy-done.6
  36.0 0.0 copy-start.7
  36.0 0.7 copy-done.7
  36.7 0.0 copy-start.3
  36.7 5.0 %block_terms.1 = (f32[16384,256]{1,0:T(8,128)S(1)}, f32[4096,256]{1,0:T(8,128)S(1)}) custom-call(s32[4,96]{1,0:T(4,128)S(1)} %bitcast.3, s32[2]{0:T(128)S(1)} %bitcast.4, bf16[16384,256]{1,0:T(8,128)(2,1)S(1)} %get-tuple-element.11.forward, bf16[4096,256]{1,0:T(8,128)(2,1)S(1)} %get-tuple-element.12.col_all, ...), custom_call_target="tpu_custom_call", output_to_operand_aliasing={{0}: (5, {}), {1}: (6, {})} | custom-call | tf_op jit(solution)/shard_map/block_terms/pallas_call | solution.py:356
  41.7 0.0 copy-start
  41.7 5.7 %copy-done = f32[16384,256]{1,0:T(8,128)} copy-done((f32[16384,256]{1,0:T(8,128)}, f32[16384,256]{1,0:T(8,128)S(1)}, u32[]{:S(2)}) %copy-start) | copy-done | bytes 16777240
  47.5 0.0 copy-done.3
  47.5 0.0 copy-start.1
  47.5 5.8 %copy-done.1 = f32[16384,256]{1,0:T(8,128)S(1)} copy-done((f32[16384,256]{1,0:T(8,128)S(1)}, f32[16384,256]{1,0:T(8,128)}, u32[]{:S(2)}) %copy-start.1) | copy-done | bytes 16777240
  53.2 0.0 copy-start.5
  53.2 41.7 %reduce_terms.1 = (f32[512,256]{1,0:T(8,128)S(1)}, f32[512,256]{1,0:T(8,128)S(1)}) custom-call(f32[16384,256]{1,0:T(8,128)S(1)} %copy-done.1, f32[4096,256]{1,0:T(8,128)S(1)} %get-tuple-element.16.acc_ref, bf16[8192,256]{1,0:T(8,128)(2,1)S(1)} %get-tuple-element.17.row_ref, f32[2,256,256]{2,1,0:T(8,128)S(1)} %copy-done.3), custom_call_target="tpu_custom_call" | custom-call | tf_op jit(solution)/shard_map/reduce_terms/pallas_call | solution.py:710
  94.9 0.0 copy-done.5
  94.9 0.8 subtract_convert_fusion
  95.7 0.9 sub.7
Async XLA Ops:
  0.6 1.0 %copy-start.2 = (f32[2,256,256]{2,1,0:T(8,128)S(1)}, f32[2,256,256]{2,1,0:T(8,128)}, u32[]{:S(2)}) copy-start(f32[2,256,256]{2,1,0:T(8,128)} %cores_ref.3) | copy-start | bytes 1572868
  1.7 0.9 copy-start.4
  35.4 0.7 copy-start.6
  36.0 0.7 copy-start.7
  36.7 10.8 %copy-start.3 = (f32[2,256,256]{2,1,0:T(8,128)S(1)}, f32[2,256,256]{2,1,0:T(8,128)}, u32[]{:S(2)}) copy-start(f32[2,256,256]{2,1,0:T(8,128)} %cores_ref.3) | copy-start | bytes 1572868
  41.7 5.7 %copy-start = (f32[16384,256]{1,0:T(8,128)}, f32[16384,256]{1,0:T(8,128)S(1)}, u32[]{:S(2)}) copy-start(f32[16384,256]{1,0:T(8,128)S(1)} %get-tuple-element.15.shared_ref) | copy-start | bytes 50331652
  47.5 5.8 %copy-start.1 = (f32[16384,256]{1,0:T(8,128)S(1)}, f32[16384,256]{1,0:T(8,128)}, u32[]{:S(2)}) copy-start(f32[16384,256]{1,0:T(8,128)} %copy-done) | copy-start | bytes 50331652
  53.2 41.7 %copy-start.5 = (bf16[512,256]{1,0:T(8,128)(2,1)S(1)}, bf16[512,256]{1,0:T(8,128)(2,1)}, u32[]{:S(2)}) copy-start(bf16[512,256]{1,0:T(8,128)(2,1)} %factor_ref.1) | copy-start | bytes 786436

commit v3 on v2

--- a/solution.py
+++ b/solution.py
@@ -89,11 +89,17 @@
             copy.wait_send()
 
 
-def greet(devices):
+def greet(devices, meanwhile=None):
     barrier = pltpu.get_barrier_semaphore()
     for device in devices:
         pl.semaphore_signal(barrier, inc=1, device_id=device, device_id_type=MESH)
+    if meanwhile is not None:
+        meanwhile()
     pl.semaphore_wait(barrier, len(devices))
+
+
+def outside(x):
+    return pltpu.with_memory_space_constraint(x, pltpu.HBM)
 
 
 def pinned(x):
@@ -101,7 +107,7 @@
 
 
 def rows(start, size):
-    return pl.ds(pl.multiple_of(start, 16), size)
+    return pl.ds(pl.multiple_of(start, 128 if size % 128 == 0 else 16), size)
 
 
 GATHER_SENDS = 40 + 8
@@ -110,11 +116,12 @@
 def gather_kernel(
     factor_ref,
     cores_ref,
-    row_ref,
+    turned_ref,
     col_ref,
     forward_ref,
     shared_ref,
     acc_ref,
+    row_ref,
     cores,
     low,
     send_sems,
@@ -187,7 +194,9 @@
 
     def widen(half, a, b):
         start = here.row_piece(**axes_of(half, a, b)) * piece + half * half_rows
-        product = dot_nn(row_ref[rows(start, half_rows)], low[...]) * (1.0 / rank)
+        arrived = row_ref[rows(start, half_rows)]
+        turned_ref[:, rows(start, half_rows)] = arrived.T
+        product = dot_nn(arrived, low[...]) * (1.0 / rank)
         for layer in range(layers):
             forward_ref[rows(layer * total_rows + start, half_rows)] = product[
                 :, layer * rank : (layer + 1) * rank
@@ -266,7 +275,7 @@
     return pl.pallas_call(
         gather_kernel,
         out_shape=(
-            pltpu.VMEM(row_shape, factor.dtype),
+            pltpu.VMEM(row_shape[::-1], factor.dtype),
             pltpu.VMEM(col_shape, factor.dtype),
             pltpu.VMEM(wide_shape, jnp.bfloat16),
             pltpu.VMEM(wide_shape, jnp.float32),
@@ -275,6 +284,7 @@
         in_specs=[anywhere, anywhere],
         out_specs=(inside,) * 5,
         scratch_shapes=[
+            pltpu.VMEM(row_shape, factor.dtype),
             pltpu.VMEM(cores.shape, jnp.float32),
             pltpu.VMEM((width, layers * width), jnp.bfloat16),
             pltpu.SemaphoreType.DMA((GATHER_SENDS,)),
@@ -289,8 +299,8 @@
 
 
 def block_kernel(
-    coords_ref,
-    counts_ref,
+    coords_hbm,
+    counts_hbm,
     forward,
     col_all,
     values_hbm,
@@ -299,10 +309,18 @@
     shared,
     col_acc,
     values,
+    coords_ref,
+    counts_ref,
     value_sems,
+    scalar_sems,
 ):
     layers, block = 2, values.shape[-1]
     total_rows = forward.shape[0] // layers
+    coords_in = pltpu.make_async_copy(coords_hbm, coords_ref, scalar_sems.at[0])
+    counts_in = pltpu.make_async_copy(counts_hbm, counts_ref, scalar_sems.at[1])
+    counts_in.start()
+    coords_in.start()
+    counts_in.wait()
     groups = [(counts_ref[layer] + GROUP - 1) // GROUP for layer in range(layers)]
     total = groups[0] + groups[1]
 
@@ -318,7 +336,12 @@
         )
 
     for step in range(DEPTH - 1):
-        value_load(jnp.int32(step)).start()
+
+        @pl.when(step < total)
+        def _():
+            value_load(jnp.int32(step)).start()
+
+    coords_in.wait()
 
     @pl.loop(0, total)
     def _(step):
@@ -352,7 +375,7 @@
 
 def local_terms(coords, counts, forward, col_all, block_values, shared, col_acc):
     block = block_values.shape[-1]
-    scalars, inside = pl.BlockSpec(memory_space=pltpu.SMEM), pl.BlockSpec(memory_space=pltpu.VMEM)
+    scalars, inside = pl.BlockSpec(memory_space=pl.ANY), pl.BlockSpec(memory_space=pltpu.VMEM)
     return pl.pallas_call(
         block_kernel,
         out_shape=(pltpu.VMEM(shared.shape, jnp.float32), pltpu.VMEM(col_acc.shape, jnp.float32)),
@@ -361,7 +384,10 @@
         input_output_aliases={5: 0, 6: 1},
         scratch_shapes=[
             pltpu.VMEM((DEPTH, GROUP, block, block), jnp.int32),
+            pltpu.SMEM(coords.shape, jnp.int32),
+            pltpu.SMEM(counts.shape, jnp.int32),
             pltpu.SemaphoreType.DMA((DEPTH,)),
+            pltpu.SemaphoreType.DMA((2,)),
         ],
         compiler_params=pltpu.CompilerParams(vmem_limit_bytes=12 * 1024 * 1024),
         name="block_terms",
@@ -369,13 +395,14 @@
 
 
 REDUCE_SENDS = 60 + 10 + 20
+ROW_ORDER = (4, 5, 3, 2, 6, 7, 1)
 PASS, SIDE = {1: 0, -1: 1}, {1: 2, -1: 4}
 
 
 def reduce_kernel(
     shared_ref,
     acc_ref,
-    row_ref,
+    turned_ref,
     cores_ref,
     grad_ref,
     core_total_ref,
@@ -390,13 +417,10 @@
     col_pair,
     col_in,
     col_out,
-    core_own,
-    core_pair,
-    core_x,
+    core_out,
+    core_in,
     core_y,
     core_z,
-    core_mid,
-    core_big,
     core_all,
     send_sems,
     recv_sems,
@@ -405,14 +429,36 @@
     here = Place()
     piece, width = grad_ref.shape
     half_rows, part_rows = piece // 2, piece // 4
-    total_rows = row_ref.shape[0]
+    total_rows = turned_ref.shape[1]
     layers, rank, _ = cores_ref.shape
     links = Copies(send_sems, recv_sems, local_sems)
     cores_in = links.local(cores_ref, cores)
-    others = [{"d" + axis: d} for axis in "xyz" for d in (1, 2, 3)]
-    greet([here.device(**shift) for shift in others] + [here.device(dcore=1)])
+    row_count = 2 * RING
+    row, col = lax.axis_index("row"), lax.axis_index("col")
+
+    def row_device(d):
+        return (lax.rem(row + d, row_count), col)
+
+    partners = [row_device(d) for d in range(1, row_count)]
+    partners += [here.device(**{"d" + axis: d}) for axis in "yz" for d in (1, 2, 3)]
+    row_part = layers * rank // row_count
+
+    def core_terms_here():
+        core_terms[...] = jnp.zeros_like(core_terms)
+        step_rows = 1024
+
+        @pl.loop(0, total_rows // step_rows)
+        def _(index):
+            start = index * step_rows
+            own = turned_ref[:, rows(start, step_rows)]
+            for layer in range(layers):
+                sums = shared_ref[rows(layer * total_rows + start, step_rows)].astype(jnp.bfloat16)
+                core_terms[pl.ds(layer * rank, rank)] += dot_nn(own, sums)
+
+        core_out[...] = core_terms[...].astype(jnp.bfloat16)
+
+    greet(partners, core_terms_here)
     halves = (0, 1)
-
     cores_in.wait()
     for layer in range(layers):
         low[layer] = cores[layer].astype(jnp.bfloat16)
@@ -498,18 +544,11 @@
         col_swap[dx] = links.send(out, col_pair.at[slot], sibling)
 
     def core_start():
-        core_terms[...] = jnp.zeros_like(core_terms)
-        step_rows = 1024
-
-        @pl.loop(0, total_rows // step_rows)
-        def _(index):
-            start = index * step_rows
-            own = row_ref[rows(start, step_rows)]
-            for layer in range(layers):
-                sums = shared_ref[rows(layer * total_rows + start, step_rows)].astype(jnp.bfloat16)
-                core_terms[pl.ds(layer * rank, rank)] += dot_tn(own, sums)
-
-        stage["swap"] = links.send(core_terms.at[rows((1 - here.core) * rank, rank)], core_pair, sibling)
+        for d in ROW_ORDER:
+            chunk = lax.rem(row + d, row_count)
+            stage["row", d] = links.send(
+                core_out.at[rows(chunk * row_part, row_part)], core_in.at[d], row_device(d)
+            )
 
     last_pass, last_in = {}, {}
 
@@ -593,97 +632,80 @@
                 + wide(col_in.at[SIDE[-1] + part])
             )
 
-    x_rows, y_rows = rank // RING, rank // RING // RING
-
-    def core_to_x():
-        stage["swap"].wait_recv()
-        core_own[...] = core_terms[rows(here.core * rank, rank)] + core_pair[...]
+    def core_to_y():
+        for d in range(1, row_count):
+            stage["row", d].wait_recv()
+        total = core_terms[rows(row * row_part, row_part)]
+        for d in range(1, row_count):
+            total += wide(core_in.at[d])
+        core_y[here.y] = total.astype(jnp.bfloat16)
         for d in (2, 1, 3):
-            chunk = lax.rem(here.x + d, RING)
-            stage["x", d] = links.send(
-                core_own.at[rows(chunk * x_rows, x_rows)], core_x.at[d], here.device(dx=d)
-            )
-
-    def core_to_y():
-        for d in (1, 2, 3):
-            stage["x", d].wait_recv()
-        core_mid[...] = (
-            core_own[rows(here.x * x_rows, x_rows)] + core_x[1] + core_x[2] + core_x[3]
-        )
-        for d in (2, 1, 3):
-            chunk = lax.rem(here.y + d, RING)
-            stage["y", d] = links.send(
-                core_mid.at[rows(chunk * y_rows, y_rows)], core_y.at[d], here.device(dy=d)
-            )
+            stage["y", d] = links.send(core_y.at[here.y], core_y.at[here.y], here.device(dy=d))
 
     def core_to_z():
         for d in (1, 2, 3):
             stage["y", d].wait_recv()
-        core_z[here.z] = core_mid[rows(here.y * y_rows, y_rows)] + core_y[1] + core_y[2] + core_y[3]
+        total = (wide(core_y.at[0]) + wide(core_y.at[1])) + (wide(core_y.at[2]) + wide(core_y.at[3]))
+        core_z[here.z] = total.astype(jnp.bfloat16)
         for d in (2, 1, 3):
             stage["z", d] = links.send(core_z.at[here.z], core_z.at[here.z], here.device(dz=d))
 
-    def core_back_y():
+    def core_back_row():
         for d in (1, 2, 3):
             stage["z", d].wait_recv()
-        spot = core_big.at[rows(here.x * x_rows + here.y * y_rows, y_rows)]
-        spot[...] = (core_z[0] + core_z[1]) + (core_z[2] + core_z[3])
+        spot = core_all.at[rows(row * row_part, row_part)]
+        spot[...] = (wide(core_z.at[0]) + wide(core_z.at[1])) + (wide(core_z.at[2]) + wide(core_z.at[3]))
         for d in (2, 1, 3):
-            stage["by", d] = links.send(spot, spot, here.device(dy=d))
-
-    def core_back_x():
-        for d in (1, 2, 3):
-            stage["by", d].wait_recv()
-        spot = core_big.at[rows(here.x * x_rows, x_rows)]
-        for d in (2, 1, 3):
-            stage["bx", d] = links.send(spot, spot, here.device(dx=d))
+            stage["bx", d] = links.send(spot, spot, row_device(2 * d))
+        stage["chip", 0] = links.send(spot, spot, sibling)
 
     def core_back_chip():
-        for d in (1, 2, 3):
+        for d in (1, 3, 2):
             stage["bx", d].wait_recv()
-        stage["chip"] = links.send(core_big, core_all, sibling)
+            from_row = lax.rem(row + 2 * (RING - d), row_count)
+            spot = core_all.at[rows(from_row * row_part, row_part)]
+            stage["chip", d] = links.send(spot, spot, sibling)
 
     def core_close():
-        stage["chip"].wait_recv()
-        core_total_ref[rows(here.core * rank, rank)] = core_big[...]
-        core_total_ref[rows((1 - here.core) * rank, rank)] = core_all[...]
-
+        for d in range(RING):
+            stage["chip", d].wait_recv()
+        core_total_ref[...] = core_all[...]
+
+    core_start()
     send_far(2)
+    send_far(1)
+    send_far(-1)
+    send_far(0)
     send_swap(2)
-    send_far(1)
+    send_swap(1)
+    send_swap(-1)
+    send_swap(0)
     send_plain(2)
-    for dx in (1, -1, 0):
-        send_swap(dx)
-    core_start()
+    core_to_y()
+    send_sum(2)
+    send_plain(1)
     col_far()
     col_plain(1)
     col_plain(-1)
-    send_sum(2)
-    core_to_x()
-    send_far(-1)
-    send_plain(1)
     send_sum(1)
-    core_to_y()
-    send_far(0)
+    core_to_z()
     send_plain(-1)
+    send_plain(0)
+    close(2)
+    last_far()
+    core_back_row()
+    send_sum(-1)
+    send_sum(0)
+    close(1)
+    last_plain(1)
+    core_back_chip()
     col_pass_on(1)
     col_pass_on(-1)
-    close(2)
-    last_far()
-    core_to_z()
-    send_sum(-1)
-    send_plain(0)
-    close(1)
-    last_plain(1)
-    core_back_y()
-    send_sum(0)
     close(-1)
     last_plain(-1)
-    core_back_x()
     last_sum(1)
     last_sum(-1)
     col_close()
-    core_back_chip()
     close(0)
     core_close()
     for half in halves:
@@ -699,8 +721,8 @@
     links.finish()
 
 
-def reduce(shared, col_acc, row_all, cores, piece):
-    width = row_all.shape[1]
+def reduce(shared, col_acc, turned, cores, piece):
+    width = turned.shape[0]
     layers = cores.shape[0]
     half_rows, part_rows = piece // 2, piece // 4
     rank = width
@@ -727,35 +749,33 @@
             pltpu.VMEM((RING, piece, width), low),
             pltpu.VMEM((6, half_rows, width), low),
             pltpu.VMEM((3, piece, width), low),
-            pltpu.VMEM((rank, width), full),
-            pltpu.VMEM((rank, width), full),
-            pltpu.VMEM((RING, rank // 4, width), full),
-            pltpu.VMEM((RING, rank // 16, width), full),
-            pltpu.VMEM((RING, rank // 16, width), full),
-            pltpu.VMEM((rank // 4, width), full),
-            pltpu.VMEM((rank, width), full),
-            pltpu.VMEM((rank, width), full),
+            pltpu.VMEM((layers * rank, width), low),
+            pltpu.VMEM((2 * RING, layers * rank // (2 * RING), width), low),
+            pltpu.VMEM((RING, layers * rank // (2 * RING), width), low),
+            pltpu.VMEM((RING, layers * rank // (2 * RING), width), low),
+            pltpu.VMEM((layers * rank, width), full),
             pltpu.SemaphoreType.DMA((REDUCE_SENDS,)),
             pltpu.SemaphoreType.DMA((REDUCE_SENDS,)),
             pltpu.SemaphoreType.DMA((1,)),
         ],
         compiler_params=pltpu.CompilerParams(
-            collective_id=1, has_side_effects=True, vmem_limit_bytes=28 * 1024 * 1024
+            collective_id=1, has_side_effects=True, vmem_limit_bytes=18 * 1024 * 1024
         ),
         name="reduce_terms",
-    )(shared, col_acc, row_all, cores)
+    )(shared, col_acc, turned, cores)
 
 
 def on_device(factor, relation_cores, block_coords, block_values, block_counts):
     slot_count = block_values.shape[3]
     cells = lax.axis_size("row") * lax.axis_size("col")
     layers = relation_cores.shape[0]
-    row_all, col_all, forward, shared, col_acc = map(pinned, gather(factor, relation_cores))
+    factor_far, cores_far = outside(factor), outside(relation_cores)
+    turned, col_all, forward, shared, col_acc = map(pinned, gather(factor_far, cores_far))
     shared, col_acc = map(
         pinned,
         local_terms(
-            block_coords.reshape(layers * 2, slot_count),
-            block_counts.reshape(layers),
+            outside(block_coords.reshape(layers * 2, slot_count)),
+            outside(block_counts.reshape(layers)),
             forward,
             col_all,
             block_values,
@@ -763,7 +783,7 @@
             col_acc,
         ),
     )
-    gradient, core_total = reduce(shared, col_acc, row_all, relation_cores, factor.shape[0])
+    gradient, core_total = reduce(shared, col_acc, turned, cores_far, factor.shape[0])
     factor_next = (factor.astype(jnp.float32) - step_factor * gradient).astype(jnp.bfloat16)
     core_total = core_total.reshape(relation_cores.shape) * (1.0 / factor.shape[1])
     cores_next = relation_cores - step_core / math.sqrt(cells * slot_count) * core_total

time: 98.2 us -> 75.3 us (0.77); the launches traced: 96.6 us -> 75.1 us
  local copies, waits for them, and re-layouts: 14.8 us -> 0.01 us
  Pallas kernels: 79.4 us -> 72.8 us
    unnamed x16 -> x4, local copies, waits for them, and re-layouts: 14.8 us -> 0.01 us
    pallas_call x1, Pallas kernels: 41.7 us -> 32.6 us  [reduce(): pl.pallas_call(reduce_kernel, out_shape=(jax.ShapeDtypeStruct((piece, wid...]
    pallas_call x1, Pallas kernels: 5.02 us -> 7.17 us  [local_terms(): pl.pallas_call(block_kernel, out_shape=(pltpu.VMEM(shared.shape, jnp.floa...]
where the time goes in v3:
time: 75.3 us; the launch traced here: 75.1 us
  Pallas kernels  72.8 us (97%)
  other arithmetic  1.66 us (2%)
    pallas_call x1, Pallas kernels, gather(): pl.pallas_call(gather_kernel, out_shape=(pltpu.VMEM(row_shape[::-1], fact...  33.1 us
    pallas_call x1, Pallas kernels, reduce(): pl.pallas_call(reduce_kernel, out_shape=(jax.ShapeDtypeStruct((piece, wid...  32.6 us
    pallas_call x1, Pallas kernels, local_terms(): pl.pallas_call(block_kernel, out_shape=(pltpu.VMEM(shared.shape, jnp.floa...  7.17 us

profile of v3, /device:TPU:0, one launch (start us, length us, event | category | flops | bytes accessed | tf_op | source)
XLA Modules:
  0.0 75.1 jit_solution(9524834498414567717)
XLA Ops:
  0.6 33.1 %gather_factor.1 = (bf16[256,8192]{1,0:T(8,128)(2,1)S(1)}, bf16[4096,256]{1,0:T(8,128)(2,1)S(1)}, bf16[16384,256]{1,0:T(8,128)(2,1)S(1)}, f32[16384,256]{1,0:T(8,128)S(1)}, f32[4096,256]{1,0:T(8,128)S(1)}) custom-call(bf16[512,256]{1,0:T(8,128)(2,1)} %factor_ref.1, f32[2,256,256]{2,1,0:T(8,128)} %cores_ref.3), custom_call_target="tpu_custom_call" | custom-call | tf_op jit(solution)/shard_map/gather_factor/pallas_call | solution.py:275
  33.7 7.2 %block_terms.1 = (f32[16384,256]{1,0:T(8,128)S(1)}, f32[4096,256]{1,0:T(8,128)S(1)}) custom-call(s32[4,96]{1,0:T(4,128)} %bitcast.4, s32[2]{0:T(128)} %bitcast.5, bf16[16384,256]{1,0:T(8,128)(2,1)S(1)} %get-tuple-element.11.forward, bf16[4096,256]{1,0:T(8,128)(2,1)S(1)} %get-tuple-element.12.col_all, ...), custom_call_target="tpu_custom_call", output_to_operand_aliasing={{0}: (5, {}), {1}: (6, {})} | custom-call | tf_op jit(solution)/shard_map/block_terms/pallas_call | solution.py:379
  40.9 0.0 copy-start.1
  40.9 0.0 copy-start
  40.9 32.6 %reduce_terms.1 = (f32[512,256]{1,0:T(8,128)S(1)}, f32[512,256]{1,0:T(8,128)S(1)}) custom-call(f32[16384,256]{1,0:T(8,128)S(1)} %get-tuple-element.15.shared_ref, f32[4096,256]{1,0:T(8,128)S(1)} %get-tuple-element.16.acc_ref, bf16[256,8192]{1,0:T(8,128)(2,1)S(1)} %get-tuple-element.17.turned_ref, f32[2,256,256]{2,1,0:T(8,128)} %cores_ref.3), custom_call_target="tpu_custom_call" | custom-call | tf_op jit(solution)/shard_map/reduce_terms/pallas_call | solution.py:732
  73.5 0.0 copy-done.1
  73.5 0.8 %subtract_convert_fusion = (bf16[512,256]{1,0:T(8,128)(2,1)}, f32[512,256]{1,0:T(8,128)S(1)}) fusion(f32[512,256]{1,0:T(8,128)S(1)} %get-tuple-element.18, bf16[512,256]{1,0:T(8,128)(2,1)S(1)} %copy-done.1, f32[512,256]{1,0:T(8,128)S(1)} %get-tuple-element.19), kind=kLoop, calls=%fused_computation | loop fusion | flops 655360 | bytes 2097152 | tf_op jit(solution)/shard_map/convert_element_type | solution.py:787
  74.3 0.0 copy-done
  74.3 0.9 %sub.7 = f32[2,256,256]{2,1,0:T(8,128)} subtract(f32[2,256,256]{2,1,0:T(8,128)S(1)} %copy-done, f32[2,256,256]{2,1,0:T(8,128)S(1)} %bitcast.3) | non-fusion elementwise | flops 131072 | bytes 1572864 | tf_op jit(solution)/shard_map/sub | solution.py:789
Async XLA Ops:
  40.9 32.6 %copy-start.1 = (bf16[512,256]{1,0:T(8,128)(2,1)S(1)}, bf16[512,256]{1,0:T(8,128)(2,1)}, u32[]{:S(2)}) copy-start(bf16[512,256]{1,0:T(8,128)(2,1)} %factor_ref.1) | copy-start | bytes 786436
  40.9 33.4 %copy-start = (f32[2,256,256]{2,1,0:T(8,128)S(1)}, f32[2,256,256]{2,1,0:T(8,128)}, u32[]{:S(2)}) copy-start(f32[2,256,256]{2,1,0:T(8,128)} %cores_ref.3) | copy-start | bytes 1572868

commit v4 on v3

--- a/solution.py
+++ b/solution.py
@@ -62,7 +62,7 @@
 class Copies:
     def __init__(self, send_sems, recv_sems, local_sems):
         self.send_sems, self.recv_sems, self.local_sems = send_sems, recv_sems, local_sems
-        self.sent, self.kept = [], 0
+        self.sent, self.kept, self.drained = [], 0, 0
 
     def send(self, src, dst, device):
         number = len(self.sent)
@@ -84,9 +84,11 @@
         copy.start()
         return copy
 
-    def finish(self):
-        for copy in self.sent:
+    def drain(self, keep=0):
+        last = len(self.sent) - keep
+        for copy in self.sent[self.drained : last]:
             copy.wait_send()
+        self.drained = max(self.drained, last)
 
 
 def greet(devices, meanwhile=None):
@@ -110,7 +112,7 @@
     return pl.ds(pl.multiple_of(start, 128 if size % 128 == 0 else 16), size)
 
 
-GATHER_SENDS = 40 + 8
+GATHER_SENDS = 60 + 8
 
 
 def gather_kernel(
@@ -148,9 +150,6 @@
             return row_ref.at[rows(start, half_rows)]
         return row_ref.at[rows(start + part * part_rows, part_rows)]
 
-    def own(half):
-        return factor_ref.at[pl.ds(half * half_rows, half_rows)]
-
     def col_region(dx, dcore, half=None):
         start = here.col_piece(dx=dx, dcore=dcore) * piece
         if half is None:
@@ -164,33 +163,70 @@
         return here.device(**axes_of(half, 0, sign))
 
     halves = (0, 1)
-    along, ahead, back = {}, {}, {}
-    for half in halves:
+    along, ahead, far, back, col_along, col_far = {}, {}, {}, {}, {}, {}
+    sibling = here.device(dcore=1)
+    across = []
+
+    def near(sign):
+        return 0 if sign == 1 else 1
+
+    def own(half, part):
+        return factor_ref.at[pl.ds(half * half_rows + part * part_rows, part_rows)]
+
+    def send_along(passed):
+        for half in halves:
+            for sign in (1, -1):
+                part = near(sign) if passed else 1 - near(sign)
+                along[half, sign, part] = links.send(
+                    own(half, part), region(half, 0, 0, part), first(half, sign)
+                )
+
+    def send_own(passed):
+        for half in halves:
+            for sign in (1, -1):
+                part = near(sign) if passed else 1 - near(sign)
+                ahead[half, 0, sign, part] = links.send(
+                    own(half, part), region(half, 0, 0, part), second(half, sign)
+                )
+
+    def spread(half, a, part):
+        spot = region(half, a, 0, part)
+        for sign in (1, -1) if part == 0 else (-1, 1):
+            ahead[half, a, sign, part] = links.send(spot, spot, second(half, sign))
+
+    def take_along(passed):
         for sign in (1, -1):
-            along[half, sign] = links.send(own(half), region(half, 0, 0), first(half, sign))
+            part = near(sign) if passed else 1 - near(sign)
+            for half in halves:
+                along[half, sign, part].wait_recv()
+                if passed:
+                    spot = region(half, -sign, 0, part)
+                    far[half, sign] = links.send(spot, spot, first(half, sign))
+                spread(half, -sign, part)
+
+    def take_far():
         for sign in (1, -1):
-            ahead[half, 0, sign] = links.send(own(half), region(half, 0, 0), second(half, sign))
-    col_along = {
-        sign: links.send(factor_ref, col_region(0, 0), here.device(dx=sign)) for sign in (1, -1)
-    }
-    sibling = here.device(dcore=1)
-    across = [links.send(factor_ref, col_region(0, 0), sibling)]
-    kept = [links.local(factor_ref, row_ref.at[rows(here.row_piece() * piece, piece)])]
-    kept.append(links.local(factor_ref, col_region(0, 0)))
-
-    zero_rows = 512
-
-    @pl.loop(0, shared_ref.shape[0] // zero_rows)
-    def _(index):
-        shared_ref[rows(index * zero_rows, zero_rows)] = jnp.zeros((zero_rows, rank), jnp.float32)
-
-    @pl.loop(0, acc_ref.shape[0] // zero_rows)
-    def _(index):
-        acc_ref[rows(index * zero_rows, zero_rows)] = jnp.zeros((zero_rows, rank), jnp.float32)
-
-    cores_in.wait()
-    for layer in range(layers):
-        low[:, layer * rank : (layer + 1) * rank] = cores[layer].astype(jnp.bfloat16)
+            for half in halves:
+                far[half, sign].wait_recv()
+                spread(half, 2, near(sign))
+
+    def pass_on(a):
+        for half in halves:
+            for sign in (1, -1):
+                part = near(sign)
+                ahead[half, a, sign, part].wait_recv()
+                spot = region(half, a, -sign, part)
+                back[half, a, sign] = links.send(spot, spot, second(half, sign))
+
+    def take_rest(a):
+        for half in halves:
+            for sign in (1, -1):
+                ahead[half, a, sign, 1 - near(sign)].wait_recv()
+
+    def take_back(a):
+        for half in halves:
+            for sign in (1, -1):
+                back[half, a, sign].wait_recv()
 
     def widen(half, a, b):
         start = here.row_piece(**axes_of(half, a, b)) * piece + half * half_rows
@@ -202,69 +238,97 @@
                 :, layer * rank : (layer + 1) * rank
             ].astype(jnp.bfloat16)
 
-    def spread(half, a):
+    def widen_all(a, b):
+        for half in halves:
+            widen(half, a, b)
+
+    def col_start():
         for sign in (1, -1):
-            ahead[half, a, sign] = links.send(region(half, a, 0), region(half, a, 0), second(half, sign))
-
-    def pass_on(half, a):
+            col_along[sign] = links.send(factor_ref, col_region(0, 0), here.device(dx=sign))
+        across.append(links.send(factor_ref, col_region(0, 0), sibling))
+
+    def col_pass():
         for sign in (1, -1):
-            ahead[half, a, sign].wait_recv()
-            part = 0 if sign == 1 else 1
-            spot = region(half, a, -sign, part)
-            back[half, a, sign] = links.send(spot, spot, second(half, sign))
-
-    def pass_wide(half, a):
+            col_along[sign].wait_recv()
+            spot = col_region(-sign, 0, near(sign))
+            col_far[sign] = links.send(spot, spot, here.device(dx=sign))
+            across.append(links.send(col_region(-sign, 0), col_region(-sign, 0), sibling))
+
+    def col_end():
         for sign in (1, -1):
-            widen(half, a, -sign)
-
-    for copy in kept:
-        copy.wait()
-    for half in halves:
-        widen(half, 0, 0)
-    far = {}
-    for sign in (1, -1):
-        for half in halves:
-            along[half, sign].wait_recv()
-            part = 0 if sign == 1 else 1
-            spot = region(half, -sign, 0, part)
-            far[half, sign] = links.send(spot, spot, first(half, sign))
-            spread(half, -sign)
-    for sign in (1, -1):
-        for half in halves:
-            widen(half, -sign, 0)
-    col_far = {}
-    for sign in (1, -1):
-        col_along[sign].wait_recv()
-        spot = col_region(-sign, 0, 0 if sign == 1 else 1)
-        col_far[sign] = links.send(spot, spot, here.device(dx=sign))
-        across.append(links.send(col_region(-sign, 0), col_region(-sign, 0), sibling))
-    for half in halves:
-        pass_on(half, 0)
-    for half in halves:
-        pass_wide(half, 0)
-    for half in halves:
-        for sign in (1, -1):
-            far[half, sign].wait_recv()
-        spread(half, 2)
-    for half in halves:
-        widen(half, 2, 0)
-    for sign in (1, -1):
-        col_far[sign].wait_recv()
-    across.append(links.send(col_region(2, 0), col_region(2, 0), sibling))
-    for a in (-1, 1, 2):
-        for half in halves:
-            pass_on(half, a)
-        for half in halves:
-            pass_wide(half, a)
-    for a in (0, -1, 1, 2):
-        for half in halves:
-            for sign in (1, -1):
-                back[half, a, sign].wait_recv()
-            widen(half, a, 2)
-    for copy in across:
-        copy.wait_recv()
-    links.finish()
-
+            col_far[sign].wait_recv()
+        across.append(links.send(col_region(2, 0), col_region(2, 0), sibling))
+
+    def prepare():
+        zero_rows = 512
+
+        @pl.loop(0, shared_ref.shape[0] // zero_rows)
+        def _(index):
+            shared_ref[rows(index * zero_rows, zero_rows)] = jnp.zeros((zero_rows, rank), jnp.float32)
+
+        @pl.loop(0, acc_ref.shape[0] // zero_rows)
+        def _(index):
+            acc_ref[rows(index * zero_rows, zero_rows)] = jnp.zeros((zero_rows, rank), jnp.float32)
+
+        cores_in.wait()
+        for layer in range(layers):
+            low[:, layer * rank : (layer + 1) * rank] = cores[layer].astype(jnp.bfloat16)
+        for copy in kept:
+            copy.wait()
+
+    def drain():
+        links.drain(4)
+
+    def finish():
+        for copy in across:
+            copy.wait_recv()
+        links.drain()
+
+    kept = [
+        links.local(factor_ref, row_ref.at[rows(here.row_piece() * piece, piece)]),
+        links.local(factor_ref, col_region(0, 0)),
+    ]
+    send_along(True)
+    send_along(False)
+    send_own(True)
+    send_own(False)
+    col_start()
+    prepare()
+    widen_all(0,0)
+    take_along(True)
+    take_along(False)
+    widen_all(-1,0)
+    widen_all(1,0)
+    col_pass()
+    take_far()
+    pass_on(0)
+    widen_all(2,0)
+    col_end()
+    take_rest(0)
+    widen_all(0,1)
+    widen_all(0,-1)
+    pass_on(-1)
+    take_rest(-1)
+    widen_all(-1,1)
+    widen_all(-1,-1)
+    pass_on(1)
+    take_rest(1)
+    widen_all(1,1)
+    widen_all(1,-1)
+    pass_on(2)
+    take_rest(2)
+    widen_all(2,1)
+    widen_all(2,-1)
+    take_back(0)
+    widen_all(0,2)
+    take_back(-1)
+    widen_all(-1,2)
+    take_back(1)
+    widen_all(1,2)
+    drain()
+    take_back(2)
+    widen_all(2,2)
+    finish()
 
 def gather(factor, cores):
     piece, width = factor.shape
@@ -445,7 +509,7 @@
 
     def core_terms_here():
         core_terms[...] = jnp.zeros_like(core_terms)
-        step_rows = 1024
+        step_rows = 8192
 
         @pl.loop(0, total_rows // step_rows)
         def _(index):
@@ -463,14 +527,11 @@
     for layer in range(layers):
         low[layer] = cores[layer].astype(jnp.bfloat16)
 
-    def term(half, a, b, part=None):
+    def term(half, a, b):
         start = here.row_piece(**axes_of(half, a, b)) * piece + half * half_rows
-        size = half_rows
-        if part is not None:
-            start, size = start + part * part_rows, part_rows
         total = None
         for layer in range(layers):
-            sums = shared_ref[rows(layer * total_rows + start, size)].astype(jnp.bfloat16)
+            sums = shared_ref[rows(layer * total_rows + start, half_rows)].astype(jnp.bfloat16)
             product = dot_nt(sums, low[layer])
             total = product if total is None else total + product
         return total * (1.0 / rank)
@@ -483,6 +544,9 @@
 
     def wide(ref):
         return ref[...].astype(jnp.float32)
+
+    def quarter(part):
+        return pl.ds(part * part_rows, part_rows)
 
     def near(sign):
         return 0 if sign == 1 else 1
@@ -505,8 +569,12 @@
         for half in halves:
             for sign in (1, -1):
                 part = 1 - near(sign)
+                both = term(half, a, sign)
                 out = row_out.at[half, a % RING, SIDE[sign] + part]
-                out[...] = term(half, a, sign, part).astype(jnp.bfloat16)
+                out[...] = both[part * part_rows : (part + 1) * part_rows].astype(jnp.bfloat16)
+                row_kept[half, a % RING, quarter(1 - part)] = both[
+                    (1 - part) * part_rows : (2 - part) * part_rows
+                ]
                 side_in[half, a, sign, part] = links.send(
                     out, row_in.at[half, a % RING, SIDE[sign] + part], second(half, sign)
                 )
@@ -515,7 +583,7 @@
         for half in halves:
             for sign in (1, -1):
                 part = near(sign)
-                mine = term(half, a, sign, part)
+                mine = row_kept[half, a % RING, quarter(part)]
                 pass_in[half, a, sign].wait_recv()
                 arrived = wide(row_in.at[half, a % RING, PASS[sign]])
                 out = row_out.at[half, a % RING, SIDE[sign] + part]
@@ -706,6 +774,7 @@
     last_sum(1)
     last_sum(-1)
     col_close()
+    links.drain(8)
     close(0)
     core_close()
     for half in halves:
@@ -718,7 +787,7 @@
                 + wide(row_in.at[half, RING, SIDE[1] + part])
                 + wide(row_in.at[half, RING, SIDE[-1] + part])
             )
-    links.finish()
+    links.drain()
 
 
 def reduce(shared, col_acc, turned, cores, piece):

time: 75.3 us -> 73.2 us (0.972)
  Pallas kernels: 72.8 us -> 70.7 us
    pallas_call x1, Pallas kernels: 33.1 us -> 30.6 us  [gather(): pl.pallas_call(gather_kernel, out_shape=(pltpu.VMEM(row_shape[::-1], fact...]
    pallas_call x1, Pallas kernels: 32.6 us -> 33.9 us  [reduce(): pl.pallas_call(reduce_kernel, out_shape=(jax.ShapeDtypeStruct((piece, wid...]
    pallas_call x1, Pallas kernels: 7.17 us -> 6.16 us  [local_terms(): pl.pallas_call(block_kernel, out_shape=(pltpu.VMEM(shared.shape, jnp.floa...]
where the time goes in v4:
time: 73.2 us; the launch traced here: 73.1 us
  Pallas kernels  70.7 us (97%)
  other arithmetic  1.66 us (2%)
    pallas_call x1, Pallas kernels, reduce(): pl.pallas_call(reduce_kernel, out_shape=(jax.ShapeDtypeStruct((piece, wid...  33.9 us
    pallas_call x1, Pallas kernels, gather(): pl.pallas_call(gather_kernel, out_shape=(pltpu.VMEM(row_shape[::-1], fact...  30.6 us
    pallas_call x1, Pallas kernels, local_terms(): pl.pallas_call(block_kernel, out_shape=(pltpu.VMEM(shared.shape, jnp.floa...  6.16 us

profile of v4, /device:TPU:0, one launch (start us, length us, event | category | flops | bytes accessed | tf_op | source)
XLA Modules:
  0.0 73.1 jit_solution(11442392700712294410)
XLA Ops:
  0.6 30.6 %gather_factor.1 = (bf16[256,8192]{1,0:T(8,128)(2,1)S(1)}, bf16[4096,256]{1,0:T(8,128)(2,1)S(1)}, bf16[16384,256]{1,0:T(8,128)(2,1)S(1)}, f32[16384,256]{1,0:T(8,128)S(1)}, f32[4096,256]{1,0:T(8,128)S(1)}) custom-call(bf16[512,256]{1,0:T(8,128)(2,1)} %factor_ref.1, f32[2,256,256]{2,1,0:T(8,128)} %cores_ref.3), custom_call_target="tpu_custom_call" | custom-call | tf_op jit(solution)/shard_map/gather_factor/pallas_call | solution.py:339
  31.3 6.2 %block_terms.1 = (f32[16384,256]{1,0:T(8,128)S(1)}, f32[4096,256]{1,0:T(8,128)S(1)}) custom-call(s32[4,96]{1,0:T(4,128)} %bitcast.4, s32[2]{0:T(128)} %bitcast.5, bf16[16384,256]{1,0:T(8,128)(2,1)S(1)} %get-tuple-element.11.forward, bf16[4096,256]{1,0:T(8,128)(2,1)S(1)} %get-tuple-element.12.col_all, ...), custom_call_target="tpu_custom_call", output_to_operand_aliasing={{0}: (5, {}), {1}: (6, {})} | custom-call | tf_op jit(solution)/shard_map/block_terms/pallas_call | solution.py:443
  37.4 0.0 copy-start.1
  37.5 0.0 copy-start
  37.5 33.9 %reduce_terms.1 = (f32[512,256]{1,0:T(8,128)S(1)}, f32[512,256]{1,0:T(8,128)S(1)}) custom-call(f32[16384,256]{1,0:T(8,128)S(1)} %get-tuple-element.15.shared_ref, f32[4096,256]{1,0:T(8,128)S(1)} %get-tuple-element.16.acc_ref, bf16[256,8192]{1,0:T(8,128)(2,1)S(1)} %get-tuple-element.17.turned_ref, f32[2,256,256]{2,1,0:T(8,128)} %cores_ref.3), custom_call_target="tpu_custom_call" | custom-call | tf_op jit(solution)/shard_map/reduce_terms/pallas_call | solution.py:801
  71.4 0.0 copy-done.1
  71.4 0.8 %subtract_convert_fusion = (bf16[512,256]{1,0:T(8,128)(2,1)}, f32[512,256]{1,0:T(8,128)S(1)}) fusion(f32[512,256]{1,0:T(8,128)S(1)} %get-tuple-element.18, bf16[512,256]{1,0:T(8,128)(2,1)S(1)} %copy-done.1, f32[512,256]{1,0:T(8,128)S(1)} %get-tuple-element.19), kind=kLoop, calls=%fused_computation | loop fusion | flops 655360 | bytes 2097152 | tf_op jit(solution)/shard_map/convert_element_type | solution.py:856
  72.2 0.0 copy-done
  72.2 0.9 %sub.7 = f32[2,256,256]{2,1,0:T(8,128)} subtract(f32[2,256,256]{2,1,0:T(8,128)S(1)} %copy-done, f32[2,256,256]{2,1,0:T(8,128)S(1)} %bitcast.3) | non-fusion elementwise | flops 131072 | bytes 1572864 | tf_op jit(solution)/shard_map/sub | solution.py:858
Async XLA Ops:
  37.4 34.0 %copy-start.1 = (bf16[512,256]{1,0:T(8,128)(2,1)S(1)}, bf16[512,256]{1,0:T(8,128)(2,1)}, u32[]{:S(2)}) copy-start(bf16[512,256]{1,0:T(8,128)(2,1)} %factor_ref.1) | copy-start | bytes 786436
  37.5 34.8 %copy-start = (f32[2,256,256]{2,1,0:T(8,128)S(1)}, f32[2,256,256]{2,1,0:T(8,128)}, u32[]{:S(2)}) copy-start(f32[2,256,256]{2,1,0:T(8,128)} %cores_ref.3) | copy-start | bytes 1572868

commit v5 on v4

--- a/solution.py
+++ b/solution.py
@@ -382,8 +382,10 @@
     total_rows = forward.shape[0] // layers
     coords_in = pltpu.make_async_copy(coords_hbm, coords_ref, scalar_sems.at[0])
     counts_in = pltpu.make_async_copy(counts_hbm, counts_ref, scalar_sems.at[1])
+    first_values = pltpu.make_async_copy(values_hbm.at[0, 0, 0, pl.ds(0, GROUP)], values.at[0], value_sems.at[0])
     counts_in.start()
     coords_in.start()
+    first_values.start()
     counts_in.wait()
     groups = [(counts_ref[layer] + GROUP - 1) // GROUP for layer in range(layers)]
     total = groups[0] + groups[1]
@@ -399,7 +401,7 @@
             values_hbm.at[layer, 0, 0, pl.ds(first_slot, GROUP)], values.at[place], value_sems.at[place]
         )
 
-    for step in range(DEPTH - 1):
+    for step in range(1, DEPTH - 1):
 
         @pl.when(step < total)
         def _():
@@ -748,15 +750,15 @@
     send_swap(1)
     send_swap(-1)
     send_swap(0)
+    core_to_y()
     send_plain(2)
-    core_to_y()
     send_sum(2)
     send_plain(1)
+    core_to_z()
     col_far()
     col_plain(1)
     col_plain(-1)
     send_sum(1)
-    core_to_z()
     send_plain(-1)
     send_plain(0)
     close(2)
@@ -764,9 +766,9 @@
     core_back_row()
     send_sum(-1)
     send_sum(0)
+    core_back_chip()
     close(1)
     last_plain(1)
-    core_back_chip()
     col_pass_on(1)
     col_pass_on(-1)
     close(-1)
@@ -775,8 +777,8 @@
     last_sum(-1)
     col_close()
     links.drain(8)
+    core_close()
     close(0)
-    core_close()
     for half in halves:
         for part in (0, 1):
             for sign in (1, -1):

time: 73.2 us -> 72 us (0.984)
  Pallas kernels: 70.7 us -> 69.6 us
where the time goes in v5:
time: 72 us; the launch traced here: 71.9 us
  Pallas kernels  69.6 us (97%)
  other arithmetic  1.66 us (2%)
    pallas_call x1, Pallas kernels, reduce(): pl.pallas_call(reduce_kernel, out_shape=(jax.ShapeDtypeStruct((piece, wid...  33.5 us
    pallas_call x1, Pallas kernels, gather(): pl.pallas_call(gather_kernel, out_shape=(pltpu.VMEM(row_shape[::-1], fact...  30.6 us
    pallas_call x1, Pallas kernels, local_terms(): pl.pallas_call(block_kernel, out_shape=(pltpu.VMEM(shared.shape, jnp.floa...  5.48 us

profile of v5, /device:TPU:0, one launch (start us, length us, event | category | flops | bytes accessed | tf_op | source)
XLA Modules:
  0.0 71.9 jit_solution(456045660687454224)
XLA Ops:
  0.6 30.6 %gather_factor.1 = (bf16[256,8192]{1,0:T(8,128)(2,1)S(1)}, bf16[4096,256]{1,0:T(8,128)(2,1)S(1)}, bf16[16384,256]{1,0:T(8,128)(2,1)S(1)}, f32[16384,256]{1,0:T(8,128)S(1)}, f32[4096,256]{1,0:T(8,128)S(1)}) custom-call(bf16[512,256]{1,0:T(8,128)(2,1)} %factor_ref.1, f32[2,256,256]{2,1,0:T(8,128)} %cores_ref.3), custom_call_target="tpu_custom_call" | custom-call | tf_op jit(solution)/shard_map/gather_factor/pallas_call | solution.py:339
  31.3 5.5 %block_terms.1 = (f32[16384,256]{1,0:T(8,128)S(1)}, f32[4096,256]{1,0:T(8,128)S(1)}) custom-call(s32[4,96]{1,0:T(4,128)} %bitcast.4, s32[2]{0:T(128)} %bitcast.5, bf16[16384,256]{1,0:T(8,128)(2,1)S(1)} %get-tuple-element.11.forward, bf16[4096,256]{1,0:T(8,128)(2,1)S(1)} %get-tuple-element.12.col_all, ...), custom_call_target="tpu_custom_call", output_to_operand_aliasing={{0}: (5, {}), {1}: (6, {})} | custom-call | tf_op jit(solution)/shard_map/block_terms/pallas_call | solution.py:445
  36.8 0.0 copy-start.1
  36.8 0.0 copy-start
  36.8 33.5 %reduce_terms.1 = (f32[512,256]{1,0:T(8,128)S(1)}, f32[512,256]{1,0:T(8,128)S(1)}) custom-call(f32[16384,256]{1,0:T(8,128)S(1)} %get-tuple-element.15.shared_ref, f32[4096,256]{1,0:T(8,128)S(1)} %get-tuple-element.16.acc_ref, bf16[256,8192]{1,0:T(8,128)(2,1)S(1)} %get-tuple-element.17.turned_ref, f32[2,256,256]{2,1,0:T(8,128)} %cores_ref.3), custom_call_target="tpu_custom_call" | custom-call | tf_op jit(solution)/shard_map/reduce_terms/pallas_call | solution.py:803
  70.2 0.0 copy-done.1
  70.3 0.8 %subtract_convert_fusion = (bf16[512,256]{1,0:T(8,128)(2,1)}, f32[512,256]{1,0:T(8,128)S(1)}) fusion(f32[512,256]{1,0:T(8,128)S(1)} %get-tuple-element.18, bf16[512,256]{1,0:T(8,128)(2,1)S(1)} %copy-done.1, f32[512,256]{1,0:T(8,128)S(1)} %get-tuple-element.19), kind=kLoop, calls=%fused_computation | loop fusion | flops 655360 | bytes 2097152 | tf_op jit(solution)/shard_map/convert_element_type | solution.py:858
  71.1 0.0 copy-done
  71.1 0.9 %sub.7 = f32[2,256,256]{2,1,0:T(8,128)} subtract(f32[2,256,256]{2,1,0:T(8,128)S(1)} %copy-done, f32[2,256,256]{2,1,0:T(8,128)S(1)} %bitcast.3) | non-fusion elementwise | flops 131072 | bytes 1572864 | tf_op jit(solution)/shard_map/sub | solution.py:860
Async XLA Ops:
  36.8 33.5 %copy-start.1 = (bf16[512,256]{1,0:T(8,128)(2,1)S(1)}, bf16[512,256]{1,0:T(8,128)(2,1)}, u32[]{:S(2)}) copy-start(bf16[512,256]{1,0:T(8,128)(2,1)} %factor_ref.1) | copy-start | bytes 786436
  36.8 34.3 %copy-start = (f32[2,256,256]{2,1,0:T(8,128)S(1)}, f32[2,256,256]{2,1,0:T(8,128)}, u32[]{:S(2)}) copy-start(f32[2,256,256]{2,1,0:T(8,128)} %cores_ref.3) | copy-start | bytes 1572868

commit v6 on v5

--- a/solution.py
+++ b/solution.py
@@ -724,7 +724,8 @@
         for d in (1, 2, 3):
             stage["z", d].wait_recv()
         spot = core_all.at[rows(row * row_part, row_part)]
-        spot[...] = (wide(core_z.at[0]) + wide(core_z.at[1])) + (wide(core_z.at[2]) + wide(core_z.at[3]))
+        total = (wide(core_z.at[0]) + wide(core_z.at[1])) + (wide(core_z.at[2]) + wide(core_z.at[3]))
+        spot[...] = total.astype(jnp.bfloat16)
         for d in (2, 1, 3):
             stage["bx", d] = links.send(spot, spot, row_device(2 * d))
         stage["chip", 0] = links.send(spot, spot, sibling)
@@ -739,7 +740,7 @@
     def core_close():
         for d in range(RING):
             stage["chip", d].wait_recv()
-        core_total_ref[...] = core_all[...]
+        core_total_ref[...] = wide(core_all)
 
     core_start()
     send_far(2)
@@ -771,14 +772,15 @@
     last_plain(1)
     col_pass_on(1)
     col_pass_on(-1)
+    links.drain(24)
     close(-1)
     last_plain(-1)
     last_sum(1)
     last_sum(-1)
     col_close()
-    links.drain(8)
     core_close()
     close(0)
+    links.drain(8)
     for half in halves:
         for part in (0, 1):
             for sign in (1, -1):
@@ -824,7 +826,7 @@
             pltpu.VMEM((2 * RING, layers * rank // (2 * RING), width), low),
             pltpu.VMEM((RING, layers * rank // (2 * RING), width), low),
             pltpu.VMEM((RING, layers * rank // (2 * RING), width), low),
-            pltpu.VMEM((layers * rank, width), full),
+            pltpu.VMEM((layers * rank, width), low),
             pltpu.SemaphoreType.DMA((REDUCE_SENDS,)),
             pltpu.SemaphoreType.DMA((REDUCE_SENDS,)),
             pltpu.SemaphoreType.DMA((1,)),

time: 72 us -> 71.8 us (level)
  no operation moved by 1% of the time
where the time goes in v6:
time: 71.8 us; the launch traced here: 72.1 us
  Pallas kernels  69.7 us (97%)
  other arithmetic  1.66 us (2%)
    pallas_call x1, Pallas kernels, reduce(): pl.pallas_call(reduce_kernel, out_shape=(jax.ShapeDtypeStruct((piece, wid...  33.6 us
    pallas_call x1, Pallas kernels, gather(): pl.pallas_call(gather_kernel, out_shape=(pltpu.VMEM(row_shape[::-1], fact...  30.6 us
    pallas_call x1, Pallas kernels, local_terms(): pl.pallas_call(block_kernel, out_shape=(pltpu.VMEM(shared.shape, jnp.floa...  5.48 us

profile of v6, /device:TPU:0, one launch (start us, length us, event | category | flops | bytes accessed | tf_op | source)
XLA Modules:
  0.0 72.1 jit_solution(2297315407209960808)
XLA Ops:
  0.6 30.6 %gather_factor.1 = (bf16[256,8192]{1,0:T(8,128)(2,1)S(1)}, bf16[4096,256]{1,0:T(8,128)(2,1)S(1)}, bf16[16384,256]{1,0:T(8,128)(2,1)S(1)}, f32[16384,256]{1,0:T(8,128)S(1)}, f32[4096,256]{1,0:T(8,128)S(1)}) custom-call(bf16[512,256]{1,0:T(8,128)(2,1)} %factor_ref.1, f32[2,256,256]{2,1,0:T(8,128)} %cores_ref.3), custom_call_target="tpu_custom_call" | custom-call | tf_op jit(solution)/shard_map/gather_factor/pallas_call | solution.py:339
  31.3 5.5 %block_terms.1 = (f32[16384,256]{1,0:T(8,128)S(1)}, f32[4096,256]{1,0:T(8,128)S(1)}) custom-call(s32[4,96]{1,0:T(4,128)} %bitcast.4, s32[2]{0:T(128)} %bitcast.5, bf16[16384,256]{1,0:T(8,128)(2,1)S(1)} %get-tuple-element.11.forward, bf16[4096,256]{1,0:T(8,128)(2,1)S(1)} %get-tuple-element.12.col_all, ...), custom_call_target="tpu_custom_call", output_to_operand_aliasing={{0}: (5, {}), {1}: (6, {})} | custom-call | tf_op jit(solution)/shard_map/block_terms/pallas_call | solution.py:445
  36.8 0.0 copy-start.1
  36.8 0.0 copy-start
  36.8 33.6 %reduce_terms.1 = (f32[512,256]{1,0:T(8,128)S(1)}, f32[512,256]{1,0:T(8,128)S(1)}) custom-call(f32[16384,256]{1,0:T(8,128)S(1)} %get-tuple-element.15.shared_ref, f32[4096,256]{1,0:T(8,128)S(1)} %get-tuple-element.16.acc_ref, bf16[256,8192]{1,0:T(8,128)(2,1)S(1)} %get-tuple-element.17.turned_ref, f32[2,256,256]{2,1,0:T(8,128)} %cores_ref.3), custom_call_target="tpu_custom_call" | custom-call | tf_op jit(solution)/shard_map/reduce_terms/pallas_call | solution.py:805
  70.4 0.0 copy-done.1
  70.4 0.8 %subtract_convert_fusion = (bf16[512,256]{1,0:T(8,128)(2,1)}, f32[512,256]{1,0:T(8,128)S(1)}) fusion(f32[512,256]{1,0:T(8,128)S(1)} %get-tuple-element.18, bf16[512,256]{1,0:T(8,128)(2,1)S(1)} %copy-done.1, f32[512,256]{1,0:T(8,128)S(1)} %get-tuple-element.19), kind=kLoop, calls=%fused_computation | loop fusion | flops 655360 | bytes 2097152 | tf_op jit(solution)/shard_map/convert_element_type | solution.py:860
  71.2 0.0 copy-done
  71.2 0.9 %sub.7 = f32[2,256,256]{2,1,0:T(8,128)} subtract(f32[2,256,256]{2,1,0:T(8,128)S(1)} %copy-done, f32[2,256,256]{2,1,0:T(8,128)S(1)} %bitcast.3) | non-fusion elementwise | flops 131072 | bytes 1572864 | tf_op jit(solution)/shard_map/sub | solution.py:862
Async XLA Ops:
  36.8 33.6 %copy-start.1 = (bf16[512,256]{1,0:T(8,128)(2,1)S(1)}, bf16[512,256]{1,0:T(8,128)(2,1)}, u32[]{:S(2)}) copy-start(bf16[512,256]{1,0:T(8,128)(2,1)} %factor_ref.1) | copy-start | bytes 786436
  36.8 34.4 %copy-start = (f32[2,256,256]{2,1,0:T(8,128)S(1)}, f32[2,256,256]{2,1,0:T(8,128)}, u32[]{:S(2)}) copy-start(f32[2,256,256]{2,1,0:T(8,128)} %cores_ref.3) | copy-start | bytes 1572868
